TPU v7x, 128 devices: a whole 4x4x4 slice. The times are simulated.
128 devices in a mesh: ctx: 32 (over x, y_hi, z), ch: 4 (over y_lo, core).
Axes of the slice: x: 4, y: 4 (y_hi: 2, y_lo: 2; y = y_hi * 2 + y_lo), z: 4, core: 2. Of those that a mesh axis runs over, the one named last changes fastest.
Arguments:
- branches: bfloat16 [3, 256, 65536], P(None, 'ch', 'ctx'), may hold values from -6 to 6
- short_taps: float32 [3, 256, 7], P(None, 'ch'), may hold values from -2 to 2
- long_filter: float32 [64, 65536], P('ch', 'ctx'), may hold values from -1.5 to 1.5
- skip_gain: float32 [256], P('ch'), may hold values from 0.5 to 1.5
Outputs:
- mixed: bfloat16 [256, 65536], P('ch', 'ctx')
All inputs are finite; a program needn't handle non-finite values.
Results may differ from a plain program's by a relative error of at most 0.0095.
Values may be sent and summed in bfloat16 or wider, within the bound.
No kernel may reach another device: no remote copies, remote signals or barrier semaphores. Data moves between devices by JAX's collectives and lax.ppermute only.
A program may use at most 128 MiB of HBM per device.

v0:
```python
import math

import jax
import jax.numpy as jnp
from jax import lax
from jax.sharding import PartitionSpec as P

highest = lax.Precision.HIGHEST


def partner(value, axis, apart):
    mask = 2**apart
    pairs = [(source, source ^ mask) for source in range(lax.axis_size(axis))]
    return lax.ppermute(value, axis, pairs)


def shifted(array, axis, by):
    size = lax.axis_size(axis)
    pairs = [(i, i + by) for i in range(size) if 0 <= i + by < size]
    return lax.ppermute(array, axis, pairs)


def twiddle_table(length, sign):
    indices = jnp.arange(length, dtype=jnp.int32)
    residue = indices[:, None] * indices[None, :] % length
    angles = sign * 2.0 * math.pi / length * residue.astype(jnp.float32)
    return (jnp.cos(angles), jnp.sin(angles))


def complex_mul(left_real, left_imag, right_real, right_imag):
    return (
        left_real * right_real - left_imag * right_imag,
        left_real * right_imag + left_imag * right_real,
    )


def split_factor(length):
    first = 1
    while first * first < length and length % (2 * first) == 0:
        first = first * 2
    return (first, length // first)


def inner_twiddle(rows_a, rows_b, length, sign):
    index_a = jnp.arange(rows_a, dtype=jnp.int32)[:, None]
    index_b = jnp.arange(rows_b, dtype=jnp.int32)[None, :]
    angles = sign * 2.0 * math.pi / length * (index_a * index_b % length).astype(jnp.float32)
    return (jnp.cos(angles), jnp.sin(angles))


def local_forward(real_part, imag_part):
    leading = real_part.shape[:-1]
    length = real_part.shape[-1]
    rows_a, rows_b = split_factor(length)
    real_part = real_part.reshape(leading + (rows_a, rows_b))
    imag_part = imag_part.reshape(leading + (rows_a, rows_b))
    cos_a, sin_a = twiddle_table(rows_a, -1.0)
    first_real = jnp.einsum("...ab,ak->...kb", real_part, cos_a, precision=highest) - jnp.einsum(
        "...ab,ak->...kb", imag_part, sin_a, precision=highest
    )
    first_imag = jnp.einsum("...ab,ak->...kb", real_part, sin_a, precision=highest) + jnp.einsum(
        "...ab,ak->...kb", imag_part, cos_a, precision=highest
    )
    turn_cos, turn_sin = inner_twiddle(rows_a, rows_b, length, -1.0)
    first_real, first_imag = complex_mul(first_real, first_imag, turn_cos, turn_sin)
    cos_b, sin_b = twiddle_table(rows_b, -1.0)
    second_real = jnp.einsum("...kb,bl->...kl", first_real, cos_b, precision=highest) - jnp.einsum(
        "...kb,bl->...kl", first_imag, sin_b, precision=highest
    )
    second_imag = jnp.einsum("...kb,bl->...kl", first_real, sin_b, precision=highest) + jnp.einsum(
        "...kb,bl->...kl", first_imag, cos_b, precision=highest
    )
    return (second_real.reshape(leading + (length,)), second_imag.reshape(leading + (length,)))


def local_inverse(real_part, imag_part):
    leading = real_part.shape[:-1]
    length = real_part.shape[-1]
    rows_a, rows_b = split_factor(length)
    real_part = real_part.reshape(leading + (rows_a, rows_b))
    imag_part = imag_part.reshape(leading + (rows_a, rows_b))
    cos_b, sin_b = twiddle_table(rows_b, 1.0)
    first_real = jnp.einsum("...kl,lb->...kb", real_part, cos_b, precision=highest) - jnp.einsum(
        "...kl,lb->...kb", imag_part, sin_b, precision=highest
    )
    first_imag = jnp.einsum("...kl,lb->...kb", real_part, sin_b, precision=highest) + jnp.einsum(
        "...kl,lb->...kb", imag_part, cos_b, precision=highest
    )
    turn_cos, turn_sin = inner_twiddle(rows_a, rows_b, length, 1.0)
    first_real, first_imag = complex_mul(first_real, first_imag, turn_cos, turn_sin)
    cos_a, sin_a = twiddle_table(rows_a, 1.0)
    second_real = jnp.einsum("...kb,ka->...ab", first_real, cos_a, precision=highest) - jnp.einsum(
        "...kb,ka->...ab", first_imag, sin_a, precision=highest
    )
    second_imag = jnp.einsum("...kb,ka->...ab", first_real, sin_a, precision=highest) + jnp.einsum(
        "...kb,ka->...ab", first_imag, cos_a, precision=highest
    )
    return (second_real.reshape(leading + (length,)), second_imag.reshape(leading + (length,)))


def block_twiddle(freqs, token_offsets, total, sign):
    angles = sign * 2.0 * math.pi / total * (freqs * token_offsets % total).astype(jnp.float32)
    return (jnp.cos(angles), jnp.sin(angles))


def reversed_index(index, levels):
    return sum(((index >> bit_pos & 1) << levels - 1 - bit_pos for bit_pos in range(levels)))


def forward_sections(real_in):
    count = lax.axis_size("ctx")
    index = lax.axis_index("ctx")
    levels = count.bit_length() - 1
    length = real_in.shape[-1]
    total = 2 * count * length
    angle = -math.pi / count * index.astype(jnp.float32)
    real_part = jnp.stack([real_in, real_in * jnp.cos(angle)], axis=1)
    imag_part = jnp.stack([jnp.zeros_like(real_in), real_in * jnp.sin(angle)], axis=1)
    for bit_pos in reversed(range(levels)):
        half = 1 << bit_pos
        peer_real, peer_imag = partner((real_part, imag_part), "ctx", bit_pos)
        upper = index >> bit_pos & 1 == 1
        turn = -math.pi / half * (index % half).astype(jnp.float32)
        diff_real, diff_imag = complex_mul(
            peer_real - real_part, peer_imag - imag_part, jnp.cos(turn), jnp.sin(turn)
        )
        real_part, imag_part = (
            jnp.where(upper, diff_real, real_part + peer_real),
            jnp.where(upper, diff_imag, imag_part + peer_imag),
        )
    freqs = 2 * reversed_index(index, levels) + jnp.arange(2, dtype=jnp.int32)[:, None]
    token_offsets = jnp.arange(length, dtype=jnp.int32)[None, :]
    turn_cos, turn_sin = block_twiddle(freqs, token_offsets, total, -1.0)
    real_part, imag_part = complex_mul(real_part, imag_part, turn_cos, turn_sin)
    return local_forward(real_part, imag_part)


def inverse_sections(real_part, imag_part):
    count = lax.axis_size("ctx")
    index = lax.axis_index("ctx")
    levels = count.bit_length() - 1
    length = real_part.shape[-1]
    total = 2 * count * length
    real_part, imag_part = local_inverse(real_part, imag_part)
    freqs = 2 * reversed_index(index, levels) + jnp.arange(2, dtype=jnp.int32)[:, None]
    token_offsets = jnp.arange(length, dtype=jnp.int32)[None, :]
    turn_cos, turn_sin = block_twiddle(freqs, token_offsets, total, 1.0)
    real_part, imag_part = complex_mul(real_part, imag_part, turn_cos, turn_sin)
    for bit_pos in range(levels):
        half = 1 << bit_pos
        upper = index >> bit_pos & 1 == 1
        turn = math.pi / half * (index % half).astype(jnp.float32)
        rotated_real, rotated_imag = complex_mul(real_part, imag_part, jnp.cos(turn), jnp.sin(turn))
        send_real = jnp.where(upper, rotated_real, real_part)
        send_imag = jnp.where(upper, rotated_imag, imag_part)
        peer_real, peer_imag = (
            partner(send_real.astype(jnp.bfloat16), "ctx", bit_pos).astype(send_real.dtype),
            partner(send_imag.astype(jnp.bfloat16), "ctx", bit_pos).astype(send_imag.dtype),
        )
        real_part = jnp.where(upper, peer_real - send_real, send_real + peer_real)
        imag_part = jnp.where(upper, peer_imag - send_imag, send_imag + peer_imag)
    angle = math.pi / count * index.astype(jnp.float32)
    combined = real_part[:, 0] + jnp.cos(angle) * real_part[:, 1] - jnp.sin(angle) * imag_part[:, 1]
    return combined / total


def on_device(branches, short_taps, long_filter, skip_gain):
    length = branches.shape[2]
    reach = short_taps.shape[2] - 1
    tail_rows = branches[:, :, length - reach :]
    previous = shifted(tail_rows, "ctx", 1)
    extended = jnp.concatenate([previous, branches], axis=2).astype(jnp.float32)
    short = sum(
        (
            short_taps[:, :, tap : tap + 1] * extended[:, :, reach - tap : reach - tap + length]
            for tap in range(reach + 1)
        )
    )
    query = short[0]
    gated = short[1] * short[2]
    signal_rows = gated.shape[0]
    transform_in, transform_out = (forward_sections, inverse_sections)
    taps = lax.all_gather(long_filter.astype(jnp.bfloat16), "ch", axis=0, tiled=True).astype(
        long_filter.dtype
    )
    spec_real, spec_imag = transform_in(jnp.concatenate([gated, taps], axis=0))
    filter_real, filter_imag = (spec_real[signal_rows:], spec_imag[signal_rows:])
    product_real, product_imag = complex_mul(
        spec_real[:signal_rows], spec_imag[:signal_rows], filter_real, filter_imag
    )
    conv = transform_out(product_real, product_imag)
    return (query * (conv + skip_gain[:, None] * gated)).astype(jnp.bfloat16)


def solution(mesh):
    placed = (P(None, "ch", "ctx"), P(None, "ch", None), P("ch", "ctx"), P("ch"))
    return jax.shard_map(
        on_device, mesh=mesh, in_specs=placed, out_specs=P("ch", "ctx"), check_vma=False
    )
```

profile of v0, /device:TPU:0, one launch (start us, length us, event | category | flops | bytes accessed | tf_op | source)
XLA Modules:
  0.0 735.3 jit_solution(15835922099739461402)
XLA Ops:
  6.8 5.8 all_gather.3
  25.5 45.0 %collective-permute-done.1 = f32[128,2,2048]{2,0,1:T(8,128)} collective-permute-done((f32[128,2,2048]{2,0,1:T(8,128)}, f32[128,2,2048]{2,0,1:T(8,128)}, u32[]{:S(2)}, u32[]{:S(2)}) %collective-permute-start.1) | collective-permute-done | bytes 2097184 | tf_op jit(solution)/shard_map/ppermute | solution.py:14
  70.4 44.4 %collective-permute-done.2 = f32[128,2,2048]{2,0,1:T(8,128)} collective-permute-done((f32[128,2,2048]{2,0,1:T(8,128)}, f32[128,2,2048]{2,0,1:T(8,128)}, u32[]{:S(2)}, u32[]{:S(2)}) %collective-permute-start.2) | collective-permute-done | bytes 2097184 | tf_op jit(solution)/shard_map/ppermute | solution.py:14
  114.8 5.2 add_select_fusion.8
  122.2 46.6 %collective-permute-done.3 = f32[128,2,2048]{2,0,1:T(8,128)S(1)} collective-permute-done((f32[128,2,2048]{2,0,1:T(8,128)}, f32[128,2,2048]{2,0,1:T(8,128)S(1)}, u32[]{:S(2)}, u32[]{:S(2)}) %collective-permute-start.3) | collective-permute-done | bytes 2097184 | tf_op jit(solution)/shard_map/ppermute | solution.py:14
  170.1 42.2 %collective-permute-done.4 = f32[128,2,2048]{2,0,1:T(8,128)} collective-permute-done((f32[128,2,2048]{2,0,1:T(8,128)}, f32[128,2,2048]{2,0,1:T(8,128)}, u32[]{:S(2)}, u32[]{:S(2)}) %collective-permute-start.4) | collective-permute-done | bytes 2097184 | tf_op jit(solution)/shard_map/ppermute | solution.py:14
  212.4 6.0 add_select_fusion.6
  222.1 46.7 %collective-permute-done.5 = f32[128,2,2048]{2,0,1:T(8,128)} collective-permute-done((f32[128,2,2048]{2,0,1:T(8,128)}, f32[128,2,2048]{2,0,1:T(8,128)}, u32[]{:S(2)}, u32[]{:S(2)}) %collective-permute-start.5) | collective-permute-done | bytes 2097184 | tf_op jit(solution)/shard_map/ppermute | solution.py:14
  268.8 42.5 %collective-permute-done.6 = f32[128,2,2048]{2,0,1:T(8,128)} collective-permute-done((f32[128,2,2048]{2,0,1:T(8,128)S(1)}, f32[128,2,2048]{2,0,1:T(8,128)}, u32[]{:S(2)}, u32[]{:S(2)}) %collective-permute-start.6) | collective-permute-done | bytes 2097184 | tf_op jit(solution)/shard_map/ppermute | solution.py:14
  311.3 6.0 add_select_fusion.4
  321.1 46.7 %collective-permute-done.7 = f32[128,2,2048]{2,0,1:T(8,128)} collective-permute-done((f32[128,2,2048]{2,0,1:T(8,128)}, f32[128,2,2048]{2,0,1:T(8,128)}, u32[]{:S(2)}, u32[]{:S(2)}) %collective-permute-start.7) | collective-permute-done | bytes 2097184 | tf_op jit(solution)/shard_map/ppermute | solution.py:14
  367.8 41.9 %collective-permute-done.8 = f32[128,2,2048]{2,0,1:T(8,128)} collective-permute-done((f32[128,2,2048]{2,0,1:T(8,128)S(1)}, f32[128,2,2048]{2,0,1:T(8,128)}, u32[]{:S(2)}, u32[]{:S(2)}) %collective-permute-start.8) | collective-permute-done | bytes 2097184 | tf_op jit(solution)/shard_map/ppermute | solution.py:14
  409.7 6.0 add_select_fusion.2
  418.6 45.8 %collective-permute-done.10 = f32[128,2,2048]{2,0,1:T(8,128)S(1)} collective-permute-done((f32[128,2,2048]{2,0,1:T(8,128)}, f32[128,2,2048]{2,0,1:T(8,128)S(1)}, u32[]{:S(2)}, u32[]{:S(2)}) %collective-permute-start.10) | collective-permute-done | bytes 2097184 | tf_op jit(solution)/shard_map/ppermute | solution.py:14
  464.5 41.1 %collective-permute-done.9 = f32[128,2,2048]{2,0,1:T(8,128)} collective-permute-done((f32[128,2,2048]{2,0,1:T(8,128)}, f32[128,2,2048]{2,0,1:T(8,128)}, u32[]{:S(2)}, u32[]{:S(2)}) %collective-permute-start.9) | collective-permute-done | bytes 2097184 | tf_op jit(solution)/shard_map/ppermute | solution.py:14
  505.6 5.6 multiply_subtract_fusion.2
  515.0 4.5 fusion.18
  526.0 4.9 fusion.24
  565.4 4.5 convolution_subtract_fusion
  574.0 6.9 fusion.2
  580.9 8.4 %fusion = f32[64,64,2,32]{1,0,3,2:T(8,128)} fusion(f32[64,2,64,32]{2,3,1,0:T(8,128)S(1)} %get-tuple-element.37), kind=kOutput, calls=%fused_computation.21 | convolution fusion | flops 201383936 | bytes 2097152 | tf_op jit(solution)/shard_map/...kb,ka->...ab/dot_general | solution.py:95
  589.3 6.9 subtract_bitcast_fusion
  600.9 8.7 %add_bitcast_fusion = f32[64,2,64,32]{0,2,3,1:T(8,128)S(1)} fusion(f32[64,64,2,32]{1,0,3,2:T(8,128)} %fusion, f32[64,2,64,32]{2,3,1,0:T(8,128)S(1)} %get-tuple-element.36), kind=kOutput, calls=%fused_computation.1 | convolution fusion | flops 201646080 | bytes 3145728 | tf_op jit(solution)/shard_map/...kb,ka->...ab/dot_general | solution.py:95
  617.6 12.7 %collective-permute-done.11 = bf16[64,2,2048]{2,0,1:T(8,128)(2,1)S(1)} collective-permute-done((bf16[64,2,2048]{2,0,1:T(8,128)(2,1)S(1)}, bf16[64,2,2048]{2,0,1:T(8,128)(2,1)S(1)}, u32[]{:S(2)}, u32[]{:S(2)}) %collective-permute-start.11) | collective-permute-done | bytes 524320 | tf_op jit(solution)/shard_map/ppermute | solution.py:14
  630.3 6.4 collective-permute-done.12
  644.2 12.7 %collective-permute-done.13 = bf16[64,2,2048]{2,0,1:T(8,128)(2,1)S(1)} collective-permute-done((bf16[64,2,2048]{2,0,1:T(8,128)(2,1)}, bf16[64,2,2048]{2,0,1:T(8,128)(2,1)S(1)}, u32[]{:S(2)}, u32[]{:S(2)}) %collective-permute-start.13) | collective-permute-done | bytes 524320 | tf_op jit(solution)/shard_map/ppermute | solution.py:14
  657.0 5.7 collective-permute-done.14
  669.3 11.7 %collective-permute-done.15 = bf16[64,2,2048]{2,0,1:T(8,128)(2,1)S(1)} collective-permute-done((bf16[64,2,2048]{2,0,1:T(8,128)(2,1)}, bf16[64,2,2048]{2,0,1:T(8,128)(2,1)S(1)}, u32[]{:S(2)}, u32[]{:S(2)}) %collective-permute-start.15) | collective-permute-done | bytes 524320 | tf_op jit(solution)/shard_map/ppermute | solution.py:14
  681.0 5.6 collective-permute-done.16
  691.9 10.5 %collective-permute-done.17 = bf16[64,2,2048]{2,0,1:T(8,128)(2,1)S(1)} collective-permute-done((bf16[64,2,2048]{2,0,1:T(8,128)(2,1)S(1)}, bf16[64,2,2048]{2,0,1:T(8,128)(2,1)S(1)}, u32[]{:S(2)}, u32[]{:S(2)}) %collective-permute-start.17) | collective-permute-done | bytes 524320 | tf_op jit(solution)/shard_map/ppermute | solution.py:14
  702.5 5.6 collective-permute-done.18
  715.8 11.4 %collective-permute-done.19 = bf16[64,2,2048]{2,0,1:T(8,128)(2,1)} collective-permute-done((bf16[64,2,2048]{2,0,1:T(8,128)(2,1)}, bf16[64,2,2048]{2,0,1:T(8,128)(2,1)}, u32[]{:S(2)}, u32[]{:S(2)}) %collective-permute-start.19) | collective-permute-done | bytes 524320 | tf_op jit(solution)/shard_map/ppermute | solution.py:14
  (98 shorter events, 128.4 us)
Async XLA Ops:
  0.0 13.7 %copy-start.9 = (bf16[3,64,2048]{2,1,0:T(8,128)(2,1)S(1)}, bf16[3,64,2048]{2,1,0:T(8,128)(2,1)}, u32[]{:S(2)}) copy-start(bf16[3,64,2048]{2,1,0:T(8,128)(2,1)} %param.4) | copy-start | bytes 2359300
  1.0 12.7 %collective-permute-start = (bf16[3,64,6]{2,1,0:T(8,128)(2,1)S(1)}, bf16[3,64,6]{2,1,0:T(8,128)(2,1)S(1)}, u32[]{:S(2)}, u32[]{:S(2)}) collective-permute-start(bf16[3,64,6]{2,1,0:T(8,128)(2,1)S(1)} %slice.80), channel_id=1, source_target_pairs={{0,4},{4,8},{8,12},{12,16},{16,20},{20,24},{24,28},{28,32},{32,36}... | collective-permute-start | bytes 6920 | tf_op jit(solution)/shard_map/ppermute | solution.py:20
  17.0 1.4 copy-start.8
  20.2 50.3 %collective-permute-start.1 = (f32[128,2,2048]{2,0,1:T(8,128)}, f32[128,2,2048]{2,0,1:T(8,128)}, u32[]{:S(2)}, u32[]{:S(2)}) collective-permute-start(f32[128,2,2048]{2,0,1:T(8,128)} %pad_maximum_fusion), channel_id=1, source_target_pairs={{0,64},{4,68},{8,72},{12,76},{16,80},{20,84},{24,88},{28,92},{32,9... | collective-permute-start | bytes 6291464 | tf_op jit(solution)/shard_map/ppermute | solution.py:14
  24.8 90.0 %collective-permute-start.2 = (f32[128,2,2048]{2,0,1:T(8,128)}, f32[128,2,2048]{2,0,1:T(8,128)}, u32[]{:S(2)}, u32[]{:S(2)}) collective-permute-start(f32[128,2,2048]{2,0,1:T(8,128)} %stack.13), channel_id=1, source_target_pairs={{0,64},{4,68},{8,72},{12,76},{16,80},{20,84},{24,88},{28,92},{32,9... | collective-permute-start | bytes 6291464 | tf_op jit(solution)/shard_map/ppermute | solution.py:14
  120.0 48.8 %collective-permute-start.3 = (f32[128,2,2048]{2,0,1:T(8,128)}, f32[128,2,2048]{2,0,1:T(8,128)S(1)}, u32[]{:S(2)}, u32[]{:S(2)}) collective-permute-start(f32[128,2,2048]{2,0,1:T(8,128)} %get-tuple-element.35), channel_id=1, source_target_pairs={{0,32},{4,36},{8,40},{12,44},{16,48},{20,52},{24,56},{28,60},{32,0... | collective-permute-start | bytes 6291464 | tf_op jit(solution)/shard_map/ppermute | solution.py:14
  121.5 90.8 %collective-permute-start.4 = (f32[128,2,2048]{2,0,1:T(8,128)}, f32[128,2,2048]{2,0,1:T(8,128)}, u32[]{:S(2)}, u32[]{:S(2)}) collective-permute-start(f32[128,2,2048]{2,0,1:T(8,128)} %get-tuple-element.34), channel_id=1, source_target_pairs={{0,32},{4,36},{8,40},{12,44},{16,48},{20,52},{24,56},{28,60},{32,0... | collective-permute-start | bytes 6291464 | tf_op jit(solution)/shard_map/ppermute | solution.py:14
  168.8 1.3 copy-start.7
  218.4 50.4 %copy-start.1 = (f32[128,2,2048]{2,0,1:T(8,128)}, f32[128,2,2048]{2,0,1:T(8,128)S(1)}, u32[]{:S(2)}) copy-start(f32[128,2,2048]{2,0,1:T(8,128)S(1)} %get-tuple-element.32) | copy-start | bytes 6291460
  218.4 50.4 %collective-permute-start.5 = (f32[128,2,2048]{2,0,1:T(8,128)}, f32[128,2,2048]{2,0,1:T(8,128)}, u32[]{:S(2)}, u32[]{:S(2)}) collective-permute-start(f32[128,2,2048]{2,0,1:T(8,128)} %get-tuple-element.33), channel_id=1, source_target_pairs={{0,16},{4,20},{8,24},{12,28},{16,0},{20,4},{24,8},{28,12},{32,48},... | collective-permute-start | bytes 6291464 | tf_op jit(solution)/shard_map/ppermute | solution.py:14
  221.5 89.8 %collective-permute-start.6 = (f32[128,2,2048]{2,0,1:T(8,128)S(1)}, f32[128,2,2048]{2,0,1:T(8,128)}, u32[]{:S(2)}, u32[]{:S(2)}) collective-permute-start(f32[128,2,2048]{2,0,1:T(8,128)S(1)} %get-tuple-element.32), channel_id=1, source_target_pairs={{0,16},{4,20},{8,24},{12,28},{16,0},{20,4},{24,8},{28,12},{32,48},... | collective-permute-start | bytes 6291464 | tf_op jit(solution)/shard_map/ppermute | solution.py:14
  317.3 50.4 %collective-permute-start.7 = (f32[128,2,2048]{2,0,1:T(8,128)}, f32[128,2,2048]{2,0,1:T(8,128)}, u32[]{:S(2)}, u32[]{:S(2)}) collective-permute-start(f32[128,2,2048]{2,0,1:T(8,128)} %get-tuple-element.31), channel_id=1, source_target_pairs={{0,8},{4,12},{8,0},{12,4},{16,24},{20,28},{24,16},{28,20},{32,40},... | collective-permute-start | bytes 6291464 | tf_op jit(solution)/shard_map/ppermute | solution.py:14
  320.9 88.8 %collective-permute-start.8 = (f32[128,2,2048]{2,0,1:T(8,128)S(1)}, f32[128,2,2048]{2,0,1:T(8,128)}, u32[]{:S(2)}, u32[]{:S(2)}) collective-permute-start(f32[128,2,2048]{2,0,1:T(8,128)S(1)} %get-tuple-element.30), channel_id=1, source_target_pairs={{0,8},{4,12},{8,0},{12,4},{16,24},{20,28},{24,16},{28,20},{32,40},... | collective-permute-start | bytes 6291464 | tf_op jit(solution)/shard_map/ppermute | solution.py:14
  415.7 48.8 %collective-permute-start.10 = (f32[128,2,2048]{2,0,1:T(8,128)}, f32[128,2,2048]{2,0,1:T(8,128)S(1)}, u32[]{:S(2)}, u32[]{:S(2)}) collective-permute-start(f32[128,2,2048]{2,0,1:T(8,128)} %get-tuple-element.28), channel_id=1, source_target_pairs={{0,4},{4,0},{8,12},{12,8},{16,20},{20,16},{24,28},{28,24},{32,36},... | collective-permute-start | bytes 6291464 | tf_op jit(solution)/shard_map/ppermute | solution.py:14
  417.3 88.3 %collective-permute-start.9 = (f32[128,2,2048]{2,0,1:T(8,128)}, f32[128,2,2048]{2,0,1:T(8,128)}, u32[]{:S(2)}, u32[]{:S(2)}) collective-permute-start(f32[128,2,2048]{2,0,1:T(8,128)} %get-tuple-element.29), channel_id=1, source_target_pairs={{0,4},{4,0},{8,12},{12,8},{16,20},{20,16},{24,28},{28,24},{32,36},... | collective-permute-start | bytes 6291464 | tf_op jit(solution)/shard_map/ppermute | solution.py:14
  526.0 4.9 copy-start.2
  565.4 4.5 copy-start
  565.4 4.5 copy-start.3
  615.4 14.9 %collective-permute-start.11 = (bf16[64,2,2048]{2,0,1:T(8,128)(2,1)S(1)}, bf16[64,2,2048]{2,0,1:T(8,128)(2,1)S(1)}, u32[]{:S(2)}, u32[]{:S(2)}) collective-permute-start(bf16[64,2,2048]{2,0,1:T(8,128)(2,1)S(1)} %get-tuple-element.21), channel_id=1, source_target_pairs={{0,4},{4,0},{8,12},{12,8},{16,20},{20,16},{24,28},{28,24},{32,36},... | collective-permute-start | bytes 1572872 | tf_op jit(solution)/shard_map/ppermute | solution.py:14
  616.8 19.9 %collective-permute-start.12 = (bf16[64,2,2048]{2,0,1:T(8,128)(2,1)S(1)}, bf16[64,2,2048]{2,0,1:T(8,128)(2,1)S(1)}, u32[]{:S(2)}, u32[]{:S(2)}) collective-permute-start(bf16[64,2,2048]{2,0,1:T(8,128)(2,1)S(1)} %get-tuple-element.50), channel_id=1, source_target_pairs={{0,4},{4,0},{8,12},{12,8},{16,20},{20,16},{24,28},{28,24},{32,36},... | collective-permute-start | bytes 1572872 | tf_op jit(solution)/shard_map/ppermute | solution.py:14
  640.6 16.4 %collective-permute-start.13 = (bf16[64,2,2048]{2,0,1:T(8,128)(2,1)}, bf16[64,2,2048]{2,0,1:T(8,128)(2,1)S(1)}, u32[]{:S(2)}, u32[]{:S(2)}) collective-permute-start(bf16[64,2,2048]{2,0,1:T(8,128)(2,1)} %get-tuple-element.17), channel_id=1, source_target_pairs={{0,8},{4,12},{8,0},{12,4},{16,24},{20,28},{24,16},{28,20},{32,40},... | collective-permute-start | bytes 1572872 | tf_op jit(solution)/shard_map/ppermute | solution.py:14
  643.3 19.3 %collective-permute-start.14 = (bf16[64,2,2048]{2,0,1:T(8,128)(2,1)S(1)}, bf16[64,2,2048]{2,0,1:T(8,128)(2,1)}, u32[]{:S(2)}, u32[]{:S(2)}) collective-permute-start(bf16[64,2,2048]{2,0,1:T(8,128)(2,1)S(1)} %get-tuple-element.48), channel_id=1, source_target_pairs={{0,8},{4,12},{8,0},{12,4},{16,24},{20,28},{24,16},{28,20},{32,40},... | collective-permute-start | bytes 1572872 | tf_op jit(solution)/shard_map/ppermute | solution.py:14
  657.0 5.7 copy-start.10
  665.6 15.4 %collective-permute-start.15 = (bf16[64,2,2048]{2,0,1:T(8,128)(2,1)}, bf16[64,2,2048]{2,0,1:T(8,128)(2,1)S(1)}, u32[]{:S(2)}, u32[]{:S(2)}) collective-permute-start(bf16[64,2,2048]{2,0,1:T(8,128)(2,1)} %get-tuple-element.13), channel_id=1, source_target_pairs={{0,16},{4,20},{8,24},{12,28},{16,0},{20,4},{24,8},{28,12},{32,48},... | collective-permute-start | bytes 1572872 | tf_op jit(solution)/shard_map/ppermute | solution.py:14
  668.8 17.8 %collective-permute-start.16 = (bf16[64,2,2048]{2,0,1:T(8,128)(2,1)}, bf16[64,2,2048]{2,0,1:T(8,128)(2,1)S(1)}, u32[]{:S(2)}, u32[]{:S(2)}) collective-permute-start(bf16[64,2,2048]{2,0,1:T(8,128)(2,1)} %get-tuple-element.46), channel_id=1, source_target_pairs={{0,16},{4,20},{8,24},{12,28},{16,0},{20,4},{24,8},{28,12},{32,48},... | collective-permute-start | bytes 1572872 | tf_op jit(solution)/shard_map/ppermute | solution.py:14
  689.7 12.7 %collective-permute-start.17 = (bf16[64,2,2048]{2,0,1:T(8,128)(2,1)S(1)}, bf16[64,2,2048]{2,0,1:T(8,128)(2,1)S(1)}, u32[]{:S(2)}, u32[]{:S(2)}) collective-permute-start(bf16[64,2,2048]{2,0,1:T(8,128)(2,1)S(1)} %get-tuple-element.9), channel_id=1, source_target_pairs={{0,32},{4,36},{8,40},{12,44},{16,48},{20,52},{24,56},{28,60},{32,0... | collective-permute-start | bytes 1572872 | tf_op jit(solution)/shard_map/ppermute | solution.py:14
  691.2 16.9 %collective-permute-start.18 = (bf16[64,2,2048]{2,0,1:T(8,128)(2,1)S(1)}, bf16[64,2,2048]{2,0,1:T(8,128)(2,1)S(1)}, u32[]{:S(2)}, u32[]{:S(2)}) collective-permute-start(bf16[64,2,2048]{2,0,1:T(8,128)(2,1)S(1)} %get-tuple-element.44), channel_id=1, source_target_pairs={{0,32},{4,36},{8,40},{12,44},{16,48},{20,52},{24,56},{28,60},{32,0... | collective-permute-start | bytes 1572872 | tf_op jit(solution)/shard_map/ppermute | solution.py:14
  702.5 5.6 copy-start.11
  712.1 20.7 %copy-start.6 = (f32[64,2048]{1,0:T(8,128)S(1)}, f32[64,2048]{1,0:T(8,128)}, u32[]{:S(2)}) copy-start(f32[64,2048]{1,0:T(8,128)} %copy-done.5) | copy-start | bytes 1572868
  712.1 20.7 %copy-start.14 = (f32[64]{0:T(128)S(1)}, f32[64]{0:T(128)}, u32[]{:S(2)}) copy-start(f32[64]{0:T(128)} %param.7) | copy-start | bytes 772
  712.1 15.1 %collective-permute-start.19 = (bf16[64,2,2048]{2,0,1:T(8,128)(2,1)}, bf16[64,2,2048]{2,0,1:T(8,128)(2,1)}, u32[]{:S(2)}, u32[]{:S(2)}) collective-permute-start(bf16[64,2,2048]{2,0,1:T(8,128)(2,1)} %get-tuple-element.7), channel_id=1, source_target_pairs={{0,64},{4,68},{8,72},{12,76},{16,80},{20,84},{24,88},{28,92},{32,9... | collective-permute-start | bytes 1572872 | tf_op jit(solution)/shard_map/ppermute | solution.py:14
  715.3 17.5 %collective-permute-start.20 = (bf16[64,2,2048]{2,0,1:T(8,128)(2,1)S(1)}, bf16[64,2,2048]{2,0,1:T(8,128)(2,1)}, u32[]{:S(2)}, u32[]{:S(2)}) collective-permute-start(bf16[64,2,2048]{2,0,1:T(8,128)(2,1)S(1)} %get-tuple-element.42), channel_id=1, source_target_pairs={{0,64},{4,68},{8,72},{12,76},{16,80},{20,84},{24,88},{28,92},{32,9... | collective-permute-start | bytes 1572872 | tf_op jit(solution)/shard_map/ppermute | solution.py:14
  (4 other events, 4.1 us)
where the time goes:
time: 743 us; the launch traced here: 735 us
  waiting for transfers between devices  530 us (71%)
  matrix products  77.7 us (10%)
  other arithmetic  60.3 us (8%)
  starting transfers between devices  33.4 us (4%)
  local copies, waits for them, and re-layouts  26.1 us (4%)
    ppermute x20, waiting for transfers between devices, partner(): return lax.ppermute(value, axis, pairs)  530 us
    ppermute x20, starting transfers between devices, partner(): return lax.ppermute(value, axis, pairs)  29.5 us
    select_n x4, other arithmetic, forward_sections(): jnp.where(upper, diff_imag, imag_part + peer_imag)  23.3 us
    convert_element_type x5, other arithmetic, inverse_sections(): send_real.astype(jnp.bfloat16)  15.4 us
  transfers between devices with their start and end apart: 21, of which 20 were waited for; matrix products, arithmetic and copies ran while one was open for 1% of the time, Pallas kernels for 0%

commit v1 on v0

v1 whole, which is shorter than its diff:
```python
import functools

import jax
import jax.numpy as jnp
from jax import lax
from jax.experimental import pallas as pl
from jax.experimental.pallas import tpu as pltpu
from jax.sharding import PartitionSpec as P

f32, bf16 = jnp.float32, jnp.bfloat16
LANES = 128
TAPS = 7
CHANNELS = 64
TOKENS = 2048
BLOCKS = TOKENS // LANES
PARTS = 32
OWN = CHANNELS // PARTS
ROWS = PARTS * BLOCKS
HALF = OWN * BLOCKS
GROUP = 8
VMEM = pl.BlockSpec(memory_space=pltpu.VMEM)


def short_kernel(branch_ref, tail_ref, taps_ref, skip_ref, filter_ref, send_ref, query_ref, direct_ref, rows_ref):
    send_ref[:, HALF:, :] = filter_ref[...]
    step = 16
    for base in range(0, CHANNELS, step):
        rows = slice(base, base + step)
        short = []
        for branch in range(3):
            own = branch_ref[branch, rows, :].astype(f32)
            extended = jnp.concatenate([tail_ref[branch, rows, :].astype(f32), own], axis=1)
            taps = taps_ref[branch, rows, :]
            total = taps[:, 0:1] * own
            for tap in range(1, TAPS):
                total += taps[:, tap : tap + 1] * extended[:, LANES - tap : LANES - tap + TOKENS]
            short.append(total)
        gated = short[1] * short[2]
        query_ref[rows, :] = short[0]
        direct_ref[rows, :] = short[0] * (skip_ref[rows, :] * gated)
        for block in range(BLOCKS):
            rows_ref[pl.ds(base * BLOCKS + block, step, stride=BLOCKS), :] = gated[
                :, block * LANES : (block + 1) * LANES
            ]
    send_ref[:, :HALF, :] = rows_ref[...].reshape(PARTS, HALF, LANES).astype(bf16)


def conv_kernel(data_ref, out_ref, signal_ref, taps_ref, left_ref, right_ref, sum_ref):
    shift = 2 * GROUP
    row = lax.broadcasted_iota(jnp.int32, (LANES, LANES), 0)
    lane = lax.broadcasted_iota(jnp.int32, (LANES, LANES), 1)
    above = lane >= row
    for own in range(OWN):
        begin = own * BLOCKS
        signal_ref[:shift, :] = jnp.zeros((shift, LANES), f32)
        signal_ref[shift:, :] = data_ref[:, begin : begin + BLOCKS, :].reshape(ROWS, LANES).astype(f32)
        taps_ref[...] = data_ref[:, HALF + begin : HALF + begin + BLOCKS, :].reshape(ROWS, LANES).astype(f32)
        for lag in range(GROUP):
            left_ref[:, lag * LANES : (lag + 1) * LANES] = signal_ref[
                shift - 2 * lag : shift - 2 * lag + ROWS, :
            ].astype(bf16)
        previous = jnp.zeros((LANES, LANES), f32)
        for group in range(ROWS // shift):
            slot = group % 2
            for lag in range(shift):
                block = group * shift + lag
                spread = jnp.broadcast_to(taps_ref[block : block + 1, :], (LANES, LANES))
                current = pltpu.roll(spread, 0, 1, stride=1, stride_axis=0)
                right_ref[
                    slot, (lag // 2) * LANES : (lag // 2 + 1) * LANES, (lag % 2) * LANES : (lag % 2 + 1) * LANES
                ] = jnp.where(above, current, previous).astype(bf16)
                previous = current
            product = jnp.dot(
                left_ref[: ROWS - shift * group, :], right_ref[slot], preferred_element_type=f32
            )
            if group == 0:
                sum_ref[shift:, :] = product
            else:
                sum_ref[shift + shift * group :, :] += product
        sum_ref[:shift, :] = jnp.zeros((shift, 2 * LANES), f32)
        result = sum_ref[shift:, :LANES] + sum_ref[shift - 1 : shift - 1 + ROWS, LANES:]
        out_ref[:, begin : begin + BLOCKS, :] = result.astype(bf16).reshape(PARTS, BLOCKS, LANES)


def mix_kernel(conv_ref, query_ref, direct_ref, out_ref, rows_ref):
    rows_ref[...] = conv_ref[...].reshape(CHANNELS * BLOCKS, LANES).astype(f32)
    for block in range(BLOCKS):
        columns = slice(block * LANES, (block + 1) * LANES)
        conv = rows_ref[pl.ds(block, CHANNELS, stride=BLOCKS), :]
        out_ref[:, columns] = (query_ref[:, columns] * conv + direct_ref[:, columns]).astype(bf16)


def on_device(branches, short_taps, long_filter, skip_gain):
    tails = lax.ppermute(branches[:, :, TOKENS - LANES :], "ctx", [(i, i + 1) for i in range(PARTS - 1)])
    filters = long_filter.reshape(long_filter.shape[0], BLOCKS, LANES).astype(bf16)
    filters = lax.all_gather(filters, "ch", axis=0, tiled=True).reshape(PARTS, HALF, LANES)
    send, query, direct = pl.pallas_call(
        short_kernel,
        out_shape=[
            jax.ShapeDtypeStruct((PARTS, 2 * HALF, LANES), bf16),
            jax.ShapeDtypeStruct((CHANNELS, TOKENS), f32),
            jax.ShapeDtypeStruct((CHANNELS, TOKENS), f32),
        ],
        in_specs=[VMEM] * 5,
        out_specs=[VMEM] * 3,
        scratch_shapes=[pltpu.VMEM((CHANNELS * BLOCKS, LANES), f32)],
        compiler_params=pltpu.CompilerParams(vmem_limit_bytes=32 * 2**20),
    )(branches, tails, short_taps, skip_gain[:, None], filters)
    data = lax.all_to_all(send, "ctx", 0, 0, tiled=True)
    conv = pl.pallas_call(
        conv_kernel,
        out_shape=jax.ShapeDtypeStruct((PARTS, HALF, LANES), bf16),
        in_specs=[VMEM],
        out_specs=VMEM,
        scratch_shapes=[
            pltpu.VMEM((2 * GROUP + ROWS, LANES), f32),
            pltpu.VMEM((ROWS, LANES), f32),
            pltpu.VMEM((ROWS, GROUP * LANES), bf16),
            pltpu.VMEM((2, GROUP * LANES, 2 * LANES), bf16),
            pltpu.VMEM((2 * GROUP + ROWS, 2 * LANES), f32),
        ],
        compiler_params=pltpu.CompilerParams(vmem_limit_bytes=32 * 2**20),
    )(data)
    conv = lax.all_to_all(conv, "ctx", 0, 0, tiled=True)
    return pl.pallas_call(
        mix_kernel,
        out_shape=jax.ShapeDtypeStruct((CHANNELS, TOKENS), bf16),
        in_specs=[VMEM] * 3,
        out_specs=VMEM,
        scratch_shapes=[pltpu.VMEM((CHANNELS * BLOCKS, LANES), f32)],
        compiler_params=pltpu.CompilerParams(vmem_limit_bytes=32 * 2**20),
    )(conv, query, direct)


def solution(mesh):
    placed = (P(None, "ch", "ctx"), P(None, "ch", None), P("ch", "ctx"), P("ch"))
    return jax.shard_map(
        on_device, mesh=mesh, in_specs=placed, out_specs=P("ch", "ctx"), check_vma=False
    )
```

time: 743 us -> 75.9 us (0.10)
  waiting for transfers between devices: 530 us -> 0.01 us
  matrix products: 77.7 us -> 0 us
  other arithmetic: 60.3 us -> 0.92 us
  blocking collectives: 5.82 us -> 44.1 us
  starting transfers between devices: 33.4 us -> 3.89 us
  Pallas kernels: 0 us -> 24.2 us
  local copies, waits for them, and re-layouts: 26.1 us -> 2.44 us
    ppermute x21 -> x1, waiting for transfers between devices: 530 us -> 0.01 us  [on_device(): lax.ppermute(branches[:, :, TOKENS - LANES:], 'ctx', [(i, i + 1) for i in...]
    dot_general x16 -> x0, matrix products: 77.7 us -> none  [the longest x1 8.71 us: local_inverse(): jnp.einsum('...kb,ka->...ab', first_real, sin_a, precision=highest)]
    all_to_all x0 -> x2, blocking collectives: none -> 38.2 us  [the longest x1 23.7 us: on_device(): data = lax.all_to_all(send, 'ctx', 0, 0, tiled=True)]
    ppermute x21 -> x1, starting transfers between devices: 33.4 us -> 3.89 us  [on_device(): lax.ppermute(branches[:, :, TOKENS - LANES:], 'ctx', [(i, i + 1) for i in...]
    select_n x5 -> x0, other arithmetic: 24.5 us -> none  [the longest x4 23.3 us: forward_sections(): jnp.where(upper, diff_imag, imag_part + peer_imag)]
    pallas_call x0 -> x3, Pallas kernels: none -> 24.2 us  [the longest x1 15.3 us: on_device(): pl.pallas_call(conv_kernel, out_shape=jax.ShapeDtypeStruct((PARTS, HALF,...]
    convert_element_type x9 -> x0, other arithmetic: 19.6 us -> none  [the longest x5 15.4 us: inverse_sections(): send_real.astype(jnp.bfloat16)]
    sub x3 -> x0, local copies, waits for them, and re-layouts: 8.01 us -> none  [the longest x2 5.43 us: complex_mul(): left_real * right_real - left_imag * right_imag]
  transfers between devices with their start and end apart: 21 -> 1, of which waited for: 20 -> 0; matrix products, arithmetic and copies ran while one was open for 1% -> 3% of each run, Pallas kernels for 0% -> 0%
where the time goes in v1:
time: 75.9 us; the launch traced here: 75.6 us
  blocking collectives  44.1 us (58%)
  Pallas kernels  24.2 us (32%)
  starting transfers between devices  3.89 us (5%)
  local copies, waits for them, and re-layouts  2.44 us (3%)
  other arithmetic  0.92 us (1%)
    all_to_all x1, blocking collectives, on_device(): data = lax.all_to_all(send, 'ctx', 0, 0, tiled=True)  23.7 us
    pallas_call x1, Pallas kernels, on_device(): pl.pallas_call(conv_kernel, out_shape=jax.ShapeDtypeStruct((PARTS, HALF,...  15.3 us
    all_to_all x1, blocking collectives, on_device(): conv = lax.all_to_all(conv, 'ctx', 0, 0, tiled=True)  14.5 us
    pallas_call x1, Pallas kernels, on_device(): pl.pallas_call(short_kernel, out_shape=[jax.ShapeDtypeStruct((PARTS, 2 *...  7.88 us
    all_gather x1, blocking collectives, on_device(): lax.all_gather(filters, 'ch', axis=0, tiled=True)  5.83 us
    ppermute x1, starting transfers between devices, on_device(): lax.ppermute(branches[:, :, TOKENS - LANES:], 'ctx', [(i, i + 1) for i in...  3.89 us
  transfers between devices with their start and end apart: 1, of which 0 were waited for; matrix products, arithmetic and copies ran while one was open for 3% of the time, Pallas kernels for 0%

profile of v1, /device:TPU:0, one launch (start us, length us, event | category | flops | bytes accessed | tf_op | source)
XLA Modules:
  0.0 75.6 jit_solution(16179216896290880940)
XLA Ops:
  0.0 0.0 copy-start
  0.0 0.9 %slice.3 = bf16[3,64,128]{2,1,0:T(8,128)(2,1)S(1)} slice(bf16[3,64,2048]{2,1,0:T(8,128)(2,1)} %branch_ref.1), slice={[0:3], [0:64], [1920:2048]} | slice | bytes 98304 | tf_op jit(solution)/shard_map/slice | solution.py:94
  0.9 3.9 %collective-permute-start = (bf16[3,64,128]{2,1,0:T(8,128)(2,1)S(1)}, bf16[3,64,128]{2,1,0:T(8,128)(2,1)S(1)}, u32[]{:S(2)}, u32[]{:S(2)}) collective-permute-start(bf16[3,64,128]{2,1,0:T(8,128)(2,1)S(1)} %slice.3), channel_id=1, source_target_pairs={{0,4},{4,8},{8,12},{12,16},{16,20},{20,24},{24,28},{28,32},{32,36}... | collective-permute-start | bytes 147464 | tf_op jit(solution)/shard_map/ppermute | solution.py:94
  4.8 0.9 %convert_bitcast_fusion = bf16[2,8,16,128]{3,1,2,0:T(8,128)(2,1)S(1)} fusion(f32[16,2048]{1,0:T(8,128)} %param.6), kind=kLoop, calls=%fused_computation | loop fusion | flops 32768 | bytes 196608
  5.7 5.8 %all_gather.3 = bf16[64,16,128]{2,1,0:T(8,128)(2,1)S(1)} all-gather(bf16[16,16,128]{2,1,0:T(8,128)(2,1)S(1)} %bitcast.6), channel_id=1, replica_groups=mesh['ctx'=32,'ch'=4] {'ch'}, dimensions={0}, use_global_device_ids=true | all-gather | bytes 327680 | tf_op jit(solution)/shard_map/all_gather | solution.py:96
  11.6 0.7 copy.8.skip_ref
  12.3 0.8 %copy.7.taps_ref = f32[3,64,7]{2,1,0:T(8,128)S(1)} copy(f32[3,64,7]{1,2,0:T(8,128)} %param.5) | data formatting | bytes 10752 | tf_op args[1]
  13.1 0.0 collective-permute-done.tail_ref
  13.1 0.0 copy-done
  13.1 7.9 %shard_map.46 = (bf16[32,64,128]{2,1,0:T(8,128)(2,1)S(1)}, f32[64,2048]{1,0:T(8,128)S(1)}, f32[64,2048]{1,0:T(8,128)S(1)}) custom-call(bf16[3,64,2048]{2,1,0:T(8,128)(2,1)S(1)} %copy-done, bf16[3,64,128]{2,1,0:T(8,128)(2,1)S(1)} %collective-permute-done.tail_ref, f32[3,64,7]{2,1,0:T(8,128)S(1)} %copy.7.taps_ref, f32[64,1]{1,0:T(8,128)S(1)} %copy.8.skip_ref, ...), custom_call_target="tpu_custom_call" | custom-call | tf_op jit(solution)/shard_map/pallas_call | solution.py:97
  21.0 23.7 %all_to_all.10.data_ref = bf16[32,64,128]{2,1,0:T(8,128)(2,1)S(1)} all-to-all(bf16[32,64,128]{2,1,0:T(8,128)(2,1)S(1)} %get-tuple-element.8), channel_id=1, replica_groups=mesh['ctx'=32,'ch'=4] {'ctx'}, dimensions={0} | all-to-all | bytes 1048576 | tf_op jit(solution)/shard_map/all_to_all | solution.py:109
  44.8 15.3 %shard_map.47 = bf16[32,32,128]{2,1,0:T(8,128)(2,1)S(1)} custom-call(bf16[32,64,128]{2,1,0:T(8,128)(2,1)S(1)} %all_to_all.10.data_ref), custom_call_target="tpu_custom_call" | custom-call | tf_op jit(solution)/shard_map/pallas_call | solution.py:110
  60.1 14.5 %all_to_all.11.conv_ref = bf16[32,32,128]{2,1,0:T(8,128)(2,1)S(1)} all-to-all(bf16[32,32,128]{2,1,0:T(8,128)(2,1)S(1)} %shard_map.47), channel_id=1, replica_groups=mesh['ctx'=32,'ch'=4] {'ctx'}, dimensions={0} | all-to-all | bytes 524288 | tf_op jit(solution)/shard_map/all_to_all | solution.py:124
  74.6 1.0 %shard_map.48 = bf16[64,2048]{1,0:T(8,128)(2,1)} custom-call(bf16[32,32,128]{2,1,0:T(8,128)(2,1)S(1)} %all_to_all.11.conv_ref, f32[64,2048]{1,0:T(8,128)S(1)} %get-tuple-element.9.query_ref, f32[64,2048]{1,0:T(8,128)S(1)} %get-tuple-element.10.direct_ref), custom_call_target="tpu_custom_call" | custom-call | tf_op jit(solution)/shard_map/pallas_call | solution.py:125
  (1 shorter events, 0.0 us)
Async XLA Ops:
  0.0 13.1 %copy-start = (bf16[3,64,2048]{2,1,0:T(8,128)(2,1)S(1)}, bf16[3,64,2048]{2,1,0:T(8,128)(2,1)}, u32[]{:S(2)}) copy-start(bf16[3,64,2048]{2,1,0:T(8,128)(2,1)} %branch_ref.1) | copy-start | bytes 2359300
  0.9 12.2 %collective-permute-start = (bf16[3,64,128]{2,1,0:T(8,128)(2,1)S(1)}, bf16[3,64,128]{2,1,0:T(8,128)(2,1)S(1)}, u32[]{:S(2)}, u32[]{:S(2)}) collective-permute-start(bf16[3,64,128]{2,1,0:T(8,128)(2,1)S(1)} %slice.3), channel_id=1, source_target_pairs={{0,4},{4,8},{8,12},{12,16},{16,20},{20,24},{24,28},{28,32},{32,36}... | collective-permute-start | bytes 147464 | tf_op jit(solution)/shard_map/ppermute | solution.py:94

commit v2 on v1

v2 whole, which is shorter than its diff:
```python
import jax
import jax.numpy as jnp
from jax import lax
from jax.experimental import pallas as pl
from jax.experimental.pallas import tpu as pltpu
from jax.sharding import PartitionSpec as P

f32, bf16 = jnp.float32, jnp.bfloat16
LANES = 128
TAPS = 7
CHANNELS = 64
TOKENS = 2048
BLOCKS = TOKENS // LANES
PARTS = 32
FILTERS = 16
OWN = CHANNELS // PARTS
ROWS = PARTS * BLOCKS
HALF = OWN * BLOCKS
GROUP = 8
WIDTH = LANES // 2
VMEM = pl.BlockSpec(memory_space=pltpu.VMEM)


def spread(taps_ref, branch, rows, count):
    taps = taps_ref[branch, rows, :]
    return [jnp.broadcast_to(taps[:, tap : tap + 1], (count, LANES)) for tap in range(TAPS)]


def short_kernel(branch_ref, taps_ref, skip_ref, rows_ref, query_ref, direct_ref):
    step = 16
    lane = lax.broadcasted_iota(jnp.int32, (step, LANES), 1)

    def body(index, carry):
        rows = pl.ds(pl.multiple_of(index * step, step), step)

        def filtered(branch):
            taps = spread(taps_ref, branch, rows, step)
            before = [jnp.zeros((step, LANES), f32)] * (TAPS - 1)
            for block in range(BLOCKS):
                own = branch_ref[branch, rows, block * LANES : (block + 1) * LANES].astype(f32)
                total = taps[0] * own
                for tap in range(1, TAPS):
                    turned = pltpu.roll(own, tap, 1)
                    total += taps[tap] * jnp.where(lane < tap, before[tap - 1], turned)
                    before[tap - 1] = turned
                yield total

        skip = jnp.broadcast_to(skip_ref[rows, :], (step, LANES))
        for block, total in enumerate(filtered(1)):
            direct_ref[rows, block * LANES : (block + 1) * LANES] = total
        for block, total in enumerate(filtered(2)):
            columns = slice(block * LANES, (block + 1) * LANES)
            gated = direct_ref[rows, columns] * total
            direct_ref[rows, columns] = skip * gated
            rows_ref[pl.ds(index * (step * BLOCKS) + block, step, stride=BLOCKS), :] = gated
        for block, total in enumerate(filtered(0)):
            columns = slice(block * LANES, (block + 1) * LANES)
            query_ref[rows, columns] = total
            direct_ref[rows, columns] = total * direct_ref[rows, columns]
        return carry

    lax.fori_loop(0, CHANNELS // step, body, 0)


def pack_kernel(
    branch_ref, tail_ref, taps_ref, skip_ref, rows_ref, own_ref, one_ref, two_ref, three_ref,
    send_ref, query_ref, direct_ref, work_ref,
):
    here = lax.axis_index("ch")
    owned = FILTERS // OWN
    for apart, taps_from in enumerate((own_ref, one_ref, two_ref, three_ref)):
        for block in range(BLOCKS):
            work_ref[pl.ds(block, FILTERS, stride=BLOCKS), :] = taps_from[:, block * LANES : (block + 1) * LANES]
        begin = pl.multiple_of((here ^ apart) * owned, owned)
        taps = work_ref[: FILTERS * BLOCKS, :].astype(bf16)
        send_ref[pl.ds(begin, owned), HALF:, :] = taps.reshape(owned, HALF, LANES)
    lane = lax.broadcasted_iota(jnp.int32, (CHANNELS, LANES), 1)
    short = []
    for branch in range(3):
        taps = spread(taps_ref, branch, slice(None), CHANNELS)
        before = tail_ref[branch].astype(f32)
        own = branch_ref[branch].astype(f32)
        total = taps[0] * own
        for tap in range(1, TAPS):
            total += taps[tap] * jnp.where(lane < tap, pltpu.roll(before, tap, 1), pltpu.roll(own, tap, 1))
        short.append(total)
    gated = short[1] * short[2]
    query_ref[...] = short[0]
    direct_ref[...] = short[0] * (skip_ref[...] * gated)
    work_ref[...] = rows_ref[...]
    work_ref[pl.ds(0, CHANNELS, stride=BLOCKS), :] = gated
    send_ref[:, :HALF, :] = work_ref[...].reshape(PARTS, HALF, LANES).astype(bf16)


def conv_kernel(data_ref, out_ref, signal_ref, taps_ref, left_ref, even_ref, odd_ref, sum_ref):
    shift = 2 * GROUP
    groups = ROWS // shift
    row = lax.broadcasted_iota(jnp.int32, (WIDTH, LANES), 0)
    lane = lax.broadcasted_iota(jnp.int32, (WIDTH, LANES), 1)
    above = lane >= row
    low = lax.broadcasted_iota(jnp.int32, (ROWS, LANES), 1) < WIDTH
    right = (even_ref, odd_ref)
    previous = jnp.zeros((WIDTH, LANES), f32)

    def load(own):
        begin = own * BLOCKS
        signal_ref[:shift, :] = jnp.zeros((shift, LANES), f32)
        signal_ref[shift:, :] = data_ref[:, begin : begin + BLOCKS, :].reshape(ROWS, LANES).astype(f32)
        taps = data_ref[:, HALF + begin : HALF + begin + BLOCKS, :]
        taps_ref[own] = taps.reshape(ROWS, LANES).astype(f32)
        for lag in range(0, GROUP, 2):
            near = signal_ref[shift - 2 * lag : shift - 2 * lag + ROWS, :]
            far = signal_ref[shift - 2 * lag - 2 : shift - 2 * lag - 2 + ROWS, :]
            columns = slice(lag * WIDTH, (lag + 2) * WIDTH)
            left_ref[own, 0, :, columns] = jnp.where(low, near, pltpu.roll(far, WIDTH, 1)).astype(bf16)
            left_ref[own, 1, :, columns] = jnp.where(low, pltpu.roll(near, WIDTH, 1), far).astype(bf16)

    def toeplitz(step, lag, previous):
        own, group = divmod(step, groups)
        block = group * shift + lag
        if block == 0:
            previous = jnp.zeros((WIDTH, LANES), f32)
        current = jnp.broadcast_to(taps_ref[own, block : block + 1, :], (WIDTH, LANES))
        current = pltpu.roll(current, 0, 1, stride=1, stride_axis=0)
        right[step % 2][
            (lag // 2) * WIDTH : (lag // 2 + 1) * WIDTH, (lag % 2) * LANES : (lag % 2 + 1) * LANES
        ] = jnp.where(above, current, previous).astype(bf16)
        return current

    def finish(own):
        sums = sum_ref.at[own]
        for half in range(2):
            sums[half, :shift, :] = jnp.zeros((shift, 2 * LANES), f32)

        def gather(half, back):
            here, there = shift - back, shift - back - 1
            return sums[half, here : here + ROWS, :LANES] + sums[half, there : there + ROWS, LANES:]

        turned = jnp.where(low, pltpu.roll(gather(1, 1), WIDTH, 1), pltpu.roll(gather(1, 0), WIDTH, 1))
        result = gather(0, 0) + turned
        out_ref[:, own * BLOCKS : (own + 1) * BLOCKS, :] = result.astype(bf16).reshape(PARTS, BLOCKS, LANES)

    for own in range(OWN):
        load(own)
    for lag in range(shift):
        previous = toeplitz(0, lag, previous)
    steps = OWN * groups
    for step in range(steps):
        own, group = divmod(step, groups)
        for half in range(2):
            if step + 1 < steps:
                for lag in range(half * GROUP, (half + 1) * GROUP):
                    previous = toeplitz(step + 1, lag, previous)
            product = jnp.dot(
                left_ref[own, half, : ROWS - shift * group, :], right[step % 2][...], preferred_element_type=f32
            )
            if group == 0:
                sum_ref[own, half, shift:, :] = product
            else:
                sum_ref[own, half, shift + shift * group :, :] += product
        if group == groups - 1:
            finish(own)


def mix_kernel(conv_ref, query_ref, direct_ref, first_query_ref, first_direct_ref, out_ref, rows_ref):
    rows_ref[...] = conv_ref[...].reshape(CHANNELS * BLOCKS, LANES).astype(f32)
    for block in range(BLOCKS):
        columns = slice(block * LANES, (block + 1) * LANES)
        conv = rows_ref[pl.ds(block, CHANNELS, stride=BLOCKS), :]
        query = query_ref[:, columns] if block else first_query_ref[...]
        direct = direct_ref[:, columns] if block else first_direct_ref[...]
        out_ref[:, columns] = (query * conv + direct).astype(bf16)


def whole(*shape):
    return pl.BlockSpec(shape, lambda i: (0,) * len(shape))


def on_device(branches, short_taps, long_filter, skip_gain):
    filters = [long_filter] + [
        lax.ppermute(long_filter, "ch", [(i, i ^ apart) for i in range(4)]) for apart in (1, 2, 3)
    ]
    tails = lax.ppermute(branches[:, :, TOKENS - LANES :], "ctx", [(i, i + 1) for i in range(PARTS - 1)])
    skip = skip_gain[:, None]
    rows, query, direct = pl.pallas_call(
        short_kernel,
        out_shape=[
            jax.ShapeDtypeStruct((CHANNELS * BLOCKS, LANES), f32),
            jax.ShapeDtypeStruct((CHANNELS, TOKENS), f32),
            jax.ShapeDtypeStruct((CHANNELS, TOKENS), f32),
        ],
        in_specs=[VMEM] * 3,
        out_specs=[VMEM] * 3,
        compiler_params=pltpu.CompilerParams(vmem_limit_bytes=16 * 2**20),
        cost_estimate=pl.CostEstimate(flops=10**7, bytes_accessed=8 * 2**20, transcendentals=0),
    )(branches, short_taps, skip)
    send, first_query, first_direct = pl.pallas_call(
        pack_kernel,
        grid=(1,),
        out_shape=[
            jax.ShapeDtypeStruct((PARTS, 2 * HALF, LANES), bf16),
            jax.ShapeDtypeStruct((CHANNELS, LANES), f32),
            jax.ShapeDtypeStruct((CHANNELS, LANES), f32),
        ],
        in_specs=[
            whole(3, CHANNELS, LANES),
            whole(3, CHANNELS, LANES),
            whole(3, CHANNELS, TAPS),
            whole(CHANNELS, 1),
            whole(CHANNELS * BLOCKS, LANES),
        ]
        + [whole(FILTERS, TOKENS)] * 4,
        out_specs=[whole(PARTS, 2 * HALF, LANES), whole(CHANNELS, LANES), whole(CHANNELS, LANES)],
        scratch_shapes=[pltpu.VMEM((CHANNELS * BLOCKS, LANES), f32)],
        compiler_params=pltpu.CompilerParams(vmem_limit_bytes=16 * 2**20),
    )(branches, tails, short_taps, skip, rows, *filters)
    data = lax.all_to_all(send, "ctx", 0, 0, tiled=True)
    conv = pl.pallas_call(
        conv_kernel,
        out_shape=jax.ShapeDtypeStruct((PARTS, HALF, LANES), bf16),
        in_specs=[VMEM],
        out_specs=VMEM,
        scratch_shapes=[
            pltpu.VMEM((2 * GROUP + ROWS, LANES), f32),
            pltpu.VMEM((OWN, ROWS, LANES), f32),
            pltpu.VMEM((OWN, 2, ROWS, GROUP * WIDTH), bf16),
            pltpu.VMEM((GROUP * WIDTH, 2 * LANES), bf16),
            pltpu.VMEM((GROUP * WIDTH, 2 * LANES), bf16),
            pltpu.VMEM((OWN, 2, 2 * GROUP + ROWS, 2 * LANES), f32),
        ],
        compiler_params=pltpu.CompilerParams(vmem_limit_bytes=32 * 2**20),
    )(data)
    conv = lax.all_to_all(conv, "ctx", 0, 0, tiled=True)
    return pl.pallas_call(
        mix_kernel,
        out_shape=jax.ShapeDtypeStruct((CHANNELS, TOKENS), bf16),
        in_specs=[VMEM] * 5,
        out_specs=VMEM,
        scratch_shapes=[pltpu.VMEM((CHANNELS * BLOCKS, LANES), f32)],
        compiler_params=pltpu.CompilerParams(vmem_limit_bytes=32 * 2**20),
    )(conv, query, direct, first_query, first_direct)


def solution(mesh):
    placed = (P(None, "ch", "ctx"), P(None, "ch", None), P("ch", "ctx"), P("ch"))
    return jax.shard_map(
        on_device, mesh=mesh, in_specs=placed, out_specs=P("ch", "ctx"), check_vma=False
    )
```

time: 75.9 us -> 61.4 us (0.81)
  Pallas kernels: 24.2 us -> 14.4 us
  blocking collectives: 44.1 us -> 37.7 us
  starting transfers between devices: 3.89 us -> 6.17 us
  other arithmetic: 0.92 us -> 0 us
    all_gather x1 -> x0, blocking collectives: 5.83 us -> none  [on_device(): lax.all_gather(filters, 'ch', axis=0, tiled=True)]
    pallas_call x1 -> x2, Pallas kernels: 7.88 us -> 2.81 us  [the longest x1 2.16 us: on_device(): pl.pallas_call(short_kernel, out_shape=[jax.ShapeDtypeStruct((CHANNELS *...]
    pallas_call x1, Pallas kernels: 15.3 us -> 10.6 us  [on_device(): pl.pallas_call(conv_kernel, out_shape=jax.ShapeDtypeStruct((PARTS, HALF,...]
    ppermute x0 -> x3, starting transfers between devices: none -> 2.14 us  [on_device(): lax.ppermute(long_filter, 'ch', [(i, i ^ apart) for i in range(4)])]
    unnamed x4 -> x9, local copies, waits for them, and re-layouts: 0.83 us -> 1.85 us
    unnamed x1 -> x0, other arithmetic: 0.92 us -> none
  transfers between devices with their start and end apart: 1 -> 4, of which waited for: 0 -> 0; matrix products, arithmetic and copies ran while one was open for 3% -> 2% of each run, Pallas kernels for 0% -> 4%
where the time goes in v2:
time: 61.4 us; the launch traced here: 61.1 us
  blocking collectives  37.7 us (61%)
  Pallas kernels  14.4 us (23%)
  starting transfers between devices  6.17 us (10%)
  local copies, waits for them, and re-layouts  2.75 us (4%)
    all_to_all x1, blocking collectives, on_device(): data = lax.all_to_all(send, 'ctx', 0, 0, tiled=True)  23.2 us
    all_to_all x1, blocking collectives, on_device(): conv = lax.all_to_all(conv, 'ctx', 0, 0, tiled=True)  14.5 us
    pallas_call x1, Pallas kernels, on_device(): pl.pallas_call(conv_kernel, out_shape=jax.ShapeDtypeStruct((PARTS, HALF,...  10.6 us
    ppermute x1, starting transfers between devices, on_device(): lax.ppermute(branches[:, :, TOKENS - LANES:], 'ctx', [(i, i + 1) for i in...  4.03 us
    pallas_call x1, Pallas kernels, on_device(): pl.pallas_call(short_kernel, out_shape=[jax.ShapeDtypeStruct((CHANNELS *...  2.16 us
    ppermute x3, starting transfers between devices, on_device(): lax.ppermute(long_filter, 'ch', [(i, i ^ apart) for i in range(4)])  2.14 us
    unnamed x9, local copies, waits for them, and re-layouts  1.85 us
  transfers between devices with their start and end apart: 4, of which 0 were waited for; matrix products, arithmetic and copies ran while one was open for 2% of the time, Pallas kernels for 4%

profile of v2, /device:TPU:0, one launch (start us, length us, event | category | flops | bytes accessed | tf_op | source)
XLA Modules:
  0.0 61.1 jit_solution(17836157808624717851)
XLA Ops:
  0.0 1.7 %collective-permute-start.2 = (f32[16,2048]{1,0:T(8,128)}, f32[16,2048]{1,0:T(8,128)S(1)}, u32[]{:S(2)}, u32[]{:S(2)}) collective-permute-start(f32[16,2048]{1,0:T(8,128)} %own_ref.1), channel_id=1, source_target_pairs={{0,2},{1,3},{2,0},{3,1},{4,6},{5,7},{6,4},{7,5},{8,10},{9,11},{10,... | collective-permute-start | bytes 393224 | tf_op jit(solution)/shard_map/ppermute | solution.py:181
  1.7 0.0 collective-permute-start.1
  1.7 0.5 collective-permute-start.3
  2.1 0.8 %slice.3 = bf16[3,64,128]{2,1,0:T(8,128)(2,1)S(1)} slice(bf16[3,64,2048]{2,1,0:T(8,128)(2,1)} %branch_ref.3), slice={[0:3], [0:64], [1920:2048]} | slice | bytes 98304 | tf_op jit(solution)/shard_map/slice | solution.py:183
  2.9 0.0 copy-start.3
  2.9 4.0 %collective-permute-start = (bf16[3,64,128]{2,1,0:T(8,128)(2,1)S(1)}, bf16[3,64,128]{2,1,0:T(8,128)(2,1)S(1)}, u32[]{:S(2)}, u32[]{:S(2)}) collective-permute-start(bf16[3,64,128]{2,1,0:T(8,128)(2,1)S(1)} %slice.3), channel_id=1, source_target_pairs={{0,4},{4,8},{8,12},{12,16},{16,20},{20,24},{24,28},{28,32},{32,36}... | collective-permute-start | bytes 147464 | tf_op jit(solution)/shard_map/ppermute | solution.py:183
  7.0 0.0 copy-done.3
  7.0 0.0 copy-start.2
  7.0 0.1 copy.8.skip_ref
  7.1 0.6 copy-done.2
  7.7 0.1 copy.7.taps_ref
  7.8 0.0 copy-start
  7.8 1.1 %copy-done = bf16[3,64,2048]{2,1,0:T(8,128)(2,1)S(1)} copy-done((bf16[3,64,2048]{2,1,0:T(8,128)(2,1)S(1)}, bf16[3,64,2048]{2,1,0:T(8,128)(2,1)}, u32[]{:S(2)}) %copy-start) | copy-done | bytes 786456
  9.0 0.0 copy-start.1
  9.0 2.2 %shard_map.46 = (f32[1024,128]{1,0:T(8,128)S(1)}, f32[64,2048]{1,0:T(8,128)S(1)}, f32[64,2048]{1,0:T(8,128)S(1)}) custom-call(bf16[3,64,2048]{2,1,0:T(8,128)(2,1)S(1)} %copy-done, f32[3,64,7]{2,1,0:T(8,128)S(1)} %copy.7.taps_ref, f32[64,1]{1,0:T(8,128)S(1)} %copy.8.skip_ref), custom_call_target="tpu_custom_call" | custom-call | flops 10000000 | bytes 8388608 | tf_op jit(solution)/shard_map/pallas_call | solution.py:185
  11.1 0.0 collective-permute-done.tail_ref
  11.1 0.0 collective-permute-done.2.two_ref
  11.1 0.0 collective-permute-done.1.one_ref
  11.2 0.0 collective-permute-done.3.three_ref
  11.2 0.0 copy-done.1
  11.2 0.6 %shard_map.47 = (bf16[32,64,128]{2,1,0:T(8,128)(2,1)S(1)}, f32[64,128]{1,0:T(8,128)S(1)}, f32[64,128]{1,0:T(8,128)S(1)}) custom-call(bf16[3,64,2048]{2,1,0:T(8,128)(2,1)S(1)} %copy-done, bf16[3,64,128]{2,1,0:T(8,128)(2,1)S(1)} %collective-permute-done.tail_ref, f32[3,64,7]{2,1,0:T(8,128)S(1)} %copy.7.taps_ref, f32[64,1]{1,0:T(8,128)S(1)} %copy.8.skip_ref, ...), custom_call_target="tpu_custom_call" | custom-call | tf_op jit(solution)/shard_map/pallas_call | solution.py:197
  11.8 23.2 %all_to_all.10.data_ref = bf16[32,64,128]{2,1,0:T(8,128)(2,1)S(1)} all-to-all(bf16[32,64,128]{2,1,0:T(8,128)(2,1)S(1)} %get-tuple-element.12), channel_id=1, replica_groups=mesh['ctx'=32,'ch'=4] {'ctx'}, dimensions={0} | all-to-all | bytes 1048576 | tf_op jit(solution)/shard_map/all_to_all | solution.py:217
  35.0 10.6 %shard_map.48 = bf16[32,32,128]{2,1,0:T(8,128)(2,1)S(1)} custom-call(bf16[32,64,128]{2,1,0:T(8,128)(2,1)S(1)} %all_to_all.10.data_ref), custom_call_target="tpu_custom_call" | custom-call | tf_op jit(solution)/shard_map/pallas_call | solution.py:218
  45.6 14.5 %all_to_all.11.conv_ref = bf16[32,32,128]{2,1,0:T(8,128)(2,1)S(1)} all-to-all(bf16[32,32,128]{2,1,0:T(8,128)(2,1)S(1)} %shard_map.48), channel_id=1, replica_groups=mesh['ctx'=32,'ch'=4] {'ctx'}, dimensions={0} | all-to-all | bytes 524288 | tf_op jit(solution)/shard_map/all_to_all | solution.py:233
  60.1 1.0 %shard_map.49 = bf16[64,2048]{1,0:T(8,128)(2,1)} custom-call(bf16[32,32,128]{2,1,0:T(8,128)(2,1)S(1)} %all_to_all.11.conv_ref, f32[64,2048]{1,0:T(8,128)S(1)} %get-tuple-element.13.query_ref, f32[64,2048]{1,0:T(8,128)S(1)} %get-tuple-element.14.direct_ref, f32[64,128]{1,0:T(8,128)S(1)} %get-tuple-element.15.first_query_ref, ...), custom_call_target="tpu_custom_call" | custom-call | tf_op jit(solution)/shard_map/pallas_call | solution.py:234
Async XLA Ops:
  0.0 11.1 %collective-permute-start.2 = (f32[16,2048]{1,0:T(8,128)}, f32[16,2048]{1,0:T(8,128)S(1)}, u32[]{:S(2)}, u32[]{:S(2)}) collective-permute-start(f32[16,2048]{1,0:T(8,128)} %own_ref.1), channel_id=1, source_target_pairs={{0,2},{1,3},{2,0},{3,1},{4,6},{5,7},{6,4},{7,5},{8,10},{9,11},{10,... | collective-permute-start | bytes 393224 | tf_op jit(solution)/shard_map/ppermute | solution.py:181
  1.7 9.5 %collective-permute-start.1 = (f32[16,2048]{1,0:T(8,128)}, f32[16,2048]{1,0:T(8,128)S(1)}, u32[]{:S(2)}, u32[]{:S(2)}) collective-permute-start(f32[16,2048]{1,0:T(8,128)} %own_ref.1), channel_id=1, source_target_pairs={{0,1},{1,0},{2,3},{3,2},{4,5},{5,4},{6,7},{7,6},{8,9},{9,8},{10,11... | collective-permute-start | bytes 393224 | tf_op jit(solution)/shard_map/ppermute | solution.py:181
  1.7 9.5 %collective-permute-start.3 = (f32[16,2048]{1,0:T(8,128)}, f32[16,2048]{1,0:T(8,128)S(1)}, u32[]{:S(2)}, u32[]{:S(2)}) collective-permute-start(f32[16,2048]{1,0:T(8,128)} %own_ref.1), channel_id=1, source_target_pairs={{0,3},{1,2},{2,1},{3,0},{4,7},{5,6},{6,5},{7,4},{8,11},{9,10},{10,... | collective-permute-start | bytes 393224 | tf_op jit(solution)/shard_map/ppermute | solution.py:181
  2.9 4.0 %copy-start.3 = (f32[64]{0:T(128)S(1)}, f32[64]{0:T(128)}, u32[]{:S(2)}) copy-start(f32[64]{0:T(128)} %param.7) | copy-start | bytes 772
  2.9 8.2 %collective-permute-start = (bf16[3,64,128]{2,1,0:T(8,128)(2,1)S(1)}, bf16[3,64,128]{2,1,0:T(8,128)(2,1)S(1)}, u32[]{:S(2)}, u32[]{:S(2)}) collective-permute-start(bf16[3,64,128]{2,1,0:T(8,128)(2,1)S(1)} %slice.3), channel_id=1, source_target_pairs={{0,4},{4,8},{8,12},{12,16},{16,20},{20,24},{24,28},{28,32},{32,36}... | collective-permute-start | bytes 147464 | tf_op jit(solution)/shard_map/ppermute | solution.py:183
  7.0 0.7 %copy-start.2 = (f32[3,64,7]{1,2,0:T(8,128)S(1)}, f32[3,64,7]{1,2,0:T(8,128)}, u32[]{:S(2)}) copy-start(f32[3,64,7]{1,2,0:T(8,128)} %param.5) | copy-start | bytes 16132
  7.8 1.1 %copy-start = (bf16[3,64,2048]{2,1,0:T(8,128)(2,1)S(1)}, bf16[3,64,2048]{2,1,0:T(8,128)(2,1)}, u32[]{:S(2)}) copy-start(bf16[3,64,2048]{2,1,0:T(8,128)(2,1)} %branch_ref.3) | copy-start | bytes 2359300
  9.0 2.2 %copy-start.1 = (f32[16,2048]{1,0:T(8,128)S(1)}, f32[16,2048]{1,0:T(8,128)}, u32[]{:S(2)}) copy-start(f32[16,2048]{1,0:T(8,128)} %own_ref.1) | copy-start | bytes 393220

commit v3 on v2

v3 whole, which is shorter than its diff:
```python
import jax
import jax.numpy as jnp
from jax import lax
from jax.experimental import pallas as pl
from jax.experimental.pallas import tpu as pltpu
from jax.sharding import PartitionSpec as P

f32, bf16 = jnp.float32, jnp.bfloat16
LANES = 128
TAPS = 7
REACH = TAPS - 1
CHANNELS = 64
TOKENS = 2048
BLOCKS = TOKENS // LANES
PARTS = 32
FILTERS = 16
OWN = CHANNELS // PARTS
ROWS = PARTS * BLOCKS
HALF = OWN * BLOCKS
EDGE = 8
LOW, SKIP = 48, 96
STEP = 16
GROUP = 8
WIDTH = LANES // 2
VMEM = pl.BlockSpec(memory_space=pltpu.VMEM)


def prepare_kernel(
    all_filters_ref, all_taps_ref, all_skip_ref, all_branches_ref, cast_ref, taps_ref, skip_ref, branches_ref,
    filters_ref, rows_ref, semaphores,
):
    sources = (all_filters_ref, all_taps_ref, all_skip_ref, all_branches_ref)
    targets = (filters_ref, taps_ref, skip_ref, branches_ref)
    copies = [
        pltpu.make_async_copy(source, target, semaphores.at[at])
        for at, (source, target) in enumerate(zip(sources, targets))
    ]
    for copy in copies:
        copy.start()
    copies[0].wait()
    for block in range(BLOCKS):
        rows_ref[pl.ds(block, FILTERS, stride=BLOCKS), :] = filters_ref[:, block * LANES : (block + 1) * LANES]
    cast_ref[...] = rows_ref[...].reshape(FILTERS, BLOCKS, LANES).astype(bf16)
    for copy in copies[1:]:
        copy.wait()


def short_kernel(
    branch_ref, taps_ref, skip_ref, signal_ref, edge_ref, query_ref, direct_ref, rows_ref, edges_ref, small_ref, columns_ref
):
    small_ref[...] = jnp.zeros(small_ref.shape, f32)
    for branch in range(3):
        small_ref[8 * branch : 8 * branch + TAPS, :CHANNELS] = taps_ref[branch]
    small_ref[24:25, :CHANNELS] = skip_ref[...]
    columns_ref[...] = small_ref[...].T
    lane = lax.broadcasted_iota(jnp.int32, (STEP, LANES), 1)
    first = lane < REACH

    def body(index, carry):
        rows = pl.ds(pl.multiple_of(index * STEP, STEP), STEP)
        columns = columns_ref[rows, :]

        def column(at):
            return jnp.broadcast_to(columns[:, at : at + 1], (STEP, LANES))

        def filtered(branch):
            taps = [column(8 * branch + tap) for tap in range(TAPS)]
            before = [jnp.zeros((STEP, LANES), f32)] * REACH
            for block in range(BLOCKS):
                own = branch_ref[branch, rows, block * LANES : (block + 1) * LANES].astype(f32)
                total = taps[0] * own
                for tap in range(1, TAPS):
                    turned = pltpu.roll(own, tap, 1)
                    total += taps[tap] * jnp.where(lane < tap, before[tap - 1], turned)
                    before[tap - 1] = turned
                if block == 0:
                    edges_ref[branch, rows, :] = total
                yield total

        skip = column(24)
        for branch in (1, 2, 0):
            for block, total in enumerate(filtered(branch)):
                at = slice(block * LANES, (block + 1) * LANES)
                if branch == 1:
                    direct_ref[rows, at] = total
                elif branch == 2:
                    gated = direct_ref[rows, at] * total
                    direct_ref[rows, at] = skip * gated
                    rows_ref[pl.ds(index * (STEP * BLOCKS) + block, STEP, stride=BLOCKS), :] = gated
                else:
                    direct = total * direct_ref[rows, at]
                    query_ref[rows, at] = total if block else jnp.where(first, 1.0, total)
                    direct_ref[rows, at] = direct if block else jnp.where(first, 0.0, direct)
        return carry

    lax.fori_loop(0, CHANNELS // STEP, body, 0)
    signal_ref[...] = rows_ref[...].reshape(PARTS, HALF, LANES).astype(bf16)
    lane = lax.broadcasted_iota(jnp.int32, (CHANNELS, LANES), 1)
    edge = jnp.zeros((CHANNELS, LANES), f32)
    for branch in range(3):
        edge += pltpu.roll(jnp.where(lane < REACH, edges_ref[branch], 0.0), 8 * branch, 1)
        place = 24 + 8 * branch
        last = branch_ref[branch, :, TOKENS - LANES :].astype(f32)
        for tap in range(1, TAPS):
            weight = columns_ref[:CHANNELS, 8 * branch + tap : 8 * branch + tap + 1]
            share = weight * pltpu.roll(last, place + tap, 1)
            edge += jnp.where((lane >= place) & (lane < place + tap), share, 0.0)
    skip = columns_ref[:CHANNELS, 24:25]
    high = edge.astype(bf16).astype(f32)
    skip_high = skip.astype(bf16).astype(f32)
    gains = jnp.where(lane < SKIP, 0.0, jnp.where(lane < SKIP + 8, skip_high, skip - skip_high))
    edges_ref[0] = high + pltpu.roll(edge - high, LOW, 1) + gains
    rows_ref[: PARTS * EDGE, :] = jnp.zeros((PARTS * EDGE, LANES), f32)
    for own in range(OWN):
        rows_ref[pl.ds(own, PARTS, stride=EDGE), :] = edges_ref[0, pl.ds(own, PARTS, stride=OWN), :]
    edge_ref[...] = rows_ref[: PARTS * EDGE, :].reshape(PARTS, EDGE, LANES).astype(bf16)


def pack_kernel(signal_ref, edge_ref, own_ref, one_ref, two_ref, three_ref, send_ref):
    send_ref[:, :HALF, :] = signal_ref[...]
    send_ref[:, 2 * HALF :, :] = edge_ref[...]
    here = lax.axis_index("ch")
    owned = FILTERS // OWN
    for apart, taps_from in enumerate((own_ref, one_ref, two_ref, three_ref)):
        begin = pl.multiple_of((here ^ apart) * owned, owned)
        send_ref[pl.ds(begin, owned), HALF : 2 * HALF, :] = taps_from[...].reshape(owned, HALF, LANES)


def conv_kernel(data_ref, out_ref, signal_ref, taps_ref, edge_ref, left_ref, even_ref, odd_ref, sum_ref):
    shift = 2 * GROUP
    groups = ROWS // shift
    row = lax.broadcasted_iota(jnp.int32, (WIDTH, LANES), 0)
    lane = lax.broadcasted_iota(jnp.int32, (WIDTH, LANES), 1)
    above = lane >= row
    low = lax.broadcasted_iota(jnp.int32, (ROWS, LANES), 1) < WIDTH
    right = (even_ref, odd_ref)
    previous = jnp.zeros((WIDTH, LANES), f32)
    first = lax.broadcasted_iota(jnp.int32, (PARTS, LANES), 1) < REACH
    start = lax.broadcasted_iota(jnp.int32, (PARTS, LANES), 0) == 0
    edge_ref[...] = data_ref[:, 2 * HALF :, :].reshape(PARTS * EDGE, LANES).astype(f32)
    opening = pl.ds(shift, PARTS, stride=BLOCKS)

    def turn_back(value, by):
        return pltpu.roll(value, LANES - by, 1)

    def edges(own):
        row = edge_ref[pl.ds(own, PARTS, stride=EDGE), :]
        share = row + turn_back(row, LOW)
        other = jnp.where(start, 0.0, pltpu.roll(turn_back(share, 24), 1, 0))
        short = share + other
        gain = turn_back(row, SKIP) + turn_back(row, SKIP + 8)
        return short, turn_back(short, 8) * turn_back(short, 16), gain

    def load(own):
        begin = own * BLOCKS
        signal_ref[:shift, :] = jnp.zeros((shift, LANES), f32)
        signal_ref[shift:, :] = data_ref[:, begin : begin + BLOCKS, :].reshape(ROWS, LANES).astype(f32)
        signal_ref[opening, :] = jnp.where(first, edges(own)[1], signal_ref[opening, :])
        taps = data_ref[:, HALF + begin : HALF + begin + BLOCKS, :]
        taps_ref[own] = taps.reshape(ROWS, LANES).astype(f32)
        for lag in range(0, GROUP, 2):
            near = signal_ref[shift - 2 * lag : shift - 2 * lag + ROWS, :]
            far = signal_ref[shift - 2 * lag - 2 : shift - 2 * lag - 2 + ROWS, :]
            columns = slice(lag * WIDTH, (lag + 2) * WIDTH)
            left_ref[own, 0, :, columns] = jnp.where(low, near, pltpu.roll(far, WIDTH, 1)).astype(bf16)
            left_ref[own, 1, :, columns] = jnp.where(low, pltpu.roll(near, WIDTH, 1), far).astype(bf16)

    def toeplitz(step, lag, previous):
        own, group = divmod(step, groups)
        block = group * shift + lag
        if block == 0:
            previous = jnp.zeros((WIDTH, LANES), f32)
        current = jnp.broadcast_to(taps_ref[own, block : block + 1, :], (WIDTH, LANES))
        current = pltpu.roll(current, 0, 1, stride=1, stride_axis=0)
        right[step % 2][
            (lag // 2) * WIDTH : (lag // 2 + 1) * WIDTH, (lag % 2) * LANES : (lag % 2 + 1) * LANES
        ] = jnp.where(above, current, previous).astype(bf16)
        return current

    def finish(own):
        sums = sum_ref.at[own]
        for half in range(2):
            sums[half, :shift, :] = jnp.zeros((shift, 2 * LANES), f32)

        def gather(half, back):
            here, there = shift - back, shift - back - 1
            return sums[half, here : here + ROWS, :LANES] + sums[half, there : there + ROWS, LANES:]

        turned = jnp.where(low, pltpu.roll(gather(1, 1), WIDTH, 1), pltpu.roll(gather(1, 0), WIDTH, 1))
        signal_ref[shift:, :] = gather(0, 0) + turned
        query, gated, gain = edges(own)
        conv = signal_ref[opening, :]
        signal_ref[opening, :] = jnp.where(first, query * (conv + gain * gated), conv)
        result = signal_ref[shift:, :].astype(bf16).reshape(PARTS, BLOCKS, LANES)
        out_ref[:, own * BLOCKS : (own + 1) * BLOCKS, :] = result

    for own in range(OWN):
        load(own)
    for lag in range(shift):
        previous = toeplitz(0, lag, previous)
    steps = OWN * groups
    for step in range(steps):
        own, group = divmod(step, groups)
        for half in range(2):
            if step + 1 < steps:
                for lag in range(half * GROUP, (half + 1) * GROUP):
                    previous = toeplitz(step + 1, lag, previous)
            product = jnp.dot(
                left_ref[own, half, : ROWS - shift * group, :], right[step % 2][...], preferred_element_type=f32
            )
            if group == 0:
                sum_ref[own, half, shift:, :] = product
            else:
                sum_ref[own, half, shift + shift * group :, :] += product
        if group == groups - 1:
            finish(own)


def mix_kernel(conv_ref, query_ref, direct_ref, out_ref, rows_ref):
    rows_ref[...] = conv_ref[...].reshape(CHANNELS * BLOCKS, LANES).astype(f32)
    for block in range(BLOCKS):
        at = slice(block * LANES, (block + 1) * LANES)
        conv = rows_ref[pl.ds(block, CHANNELS, stride=BLOCKS), :]
        out_ref[:, at] = (query_ref[:, at] * conv + direct_ref[:, at]).astype(bf16)


def in_hbm(array):
    return pltpu.with_memory_space_constraint(array, pltpu.HBM)


def on_device(branches, short_taps, long_filter, skip_gain):
    own_filters, taps, skip, branches = pl.pallas_call(
        prepare_kernel,
        out_shape=[
            jax.ShapeDtypeStruct((FILTERS, BLOCKS, LANES), bf16),
            jax.ShapeDtypeStruct((3, TAPS, CHANNELS), f32),
            jax.ShapeDtypeStruct((1, CHANNELS), f32),
            jax.ShapeDtypeStruct((3, CHANNELS, TOKENS), bf16),
        ],
        in_specs=[pl.BlockSpec(memory_space=pltpu.HBM)] * 4,
        out_specs=[VMEM] * 4,
        scratch_shapes=[
            pltpu.VMEM((FILTERS, TOKENS), f32),
            pltpu.VMEM((FILTERS * BLOCKS, LANES), f32),
            pltpu.SemaphoreType.DMA((4,)),
        ],
        compiler_params=pltpu.CompilerParams(vmem_limit_bytes=8 * 2**20),
    )(in_hbm(long_filter), in_hbm(short_taps.transpose(0, 2, 1)), in_hbm(skip_gain[None, :]), in_hbm(branches))
    filters = [own_filters] + [
        lax.ppermute(own_filters, "ch", [(i, i ^ apart) for i in range(4)]) for apart in (1, 2, 3)
    ]
    signal, edge, query, direct = pl.pallas_call(
        short_kernel,
        out_shape=[
            jax.ShapeDtypeStruct((PARTS, HALF, LANES), bf16),
            jax.ShapeDtypeStruct((PARTS, EDGE, LANES), bf16),
            jax.ShapeDtypeStruct((CHANNELS, TOKENS), f32),
            jax.ShapeDtypeStruct((CHANNELS, TOKENS), f32),
        ],
        in_specs=[VMEM] * 3,
        out_specs=[VMEM] * 4,
        scratch_shapes=[
            pltpu.VMEM((CHANNELS * BLOCKS, LANES), f32),
            pltpu.VMEM((3, CHANNELS, LANES), f32),
            pltpu.VMEM((LANES, LANES), f32),
            pltpu.VMEM((LANES, LANES), f32),
        ],
        compiler_params=pltpu.CompilerParams(vmem_limit_bytes=16 * 2**20),
        cost_estimate=pl.CostEstimate(flops=10**7, bytes_accessed=8 * 2**20, transcendentals=0),
    )(branches, taps, skip)
    send = pl.pallas_call(
        pack_kernel,
        out_shape=jax.ShapeDtypeStruct((PARTS, 2 * HALF + EDGE, LANES), bf16),
        in_specs=[VMEM] * 6,
        out_specs=VMEM,
        compiler_params=pltpu.CompilerParams(vmem_limit_bytes=16 * 2**20),
    )(signal, edge, *filters)
    data = lax.all_to_all(send, "ctx", 0, 0, tiled=True)
    conv = pl.pallas_call(
        conv_kernel,
        out_shape=jax.ShapeDtypeStruct((PARTS, HALF, LANES), bf16),
        in_specs=[VMEM],
        out_specs=VMEM,
        scratch_shapes=[
            pltpu.VMEM((2 * GROUP + ROWS, LANES), f32),
            pltpu.VMEM((OWN, ROWS, LANES), f32),
            pltpu.VMEM((PARTS * EDGE, LANES), f32),
            pltpu.VMEM((OWN, 2, ROWS, GROUP * WIDTH), bf16),
            pltpu.VMEM((GROUP * WIDTH, 2 * LANES), bf16),
            pltpu.VMEM((GROUP * WIDTH, 2 * LANES), bf16),
            pltpu.VMEM((OWN, 2, 2 * GROUP + ROWS, 2 * LANES), f32),
        ],
        compiler_params=pltpu.CompilerParams(vmem_limit_bytes=32 * 2**20),
    )(data)
    conv = lax.all_to_all(conv, "ctx", 0, 0, tiled=True)
    return pl.pallas_call(
        mix_kernel,
        out_shape=jax.ShapeDtypeStruct((CHANNELS, TOKENS), bf16),
        in_specs=[VMEM] * 3,
        out_specs=VMEM,
        scratch_shapes=[pltpu.VMEM((CHANNELS * BLOCKS, LANES), f32)],
        compiler_params=pltpu.CompilerParams(vmem_limit_bytes=32 * 2**20),
    )(conv, query, direct)


def solution(mesh):
    placed = (P(None, "ch", "ctx"), P(None, "ch", None), P("ch", "ctx"), P("ch"))
    return jax.shard_map(
        on_device, mesh=mesh, in_specs=placed, out_specs=P("ch", "ctx"), check_vma=False
    )
```

time: 61.4 us -> 58.6 us (0.954)
  starting transfers between devices: 6.17 us -> 1.95 us
  local copies, waits for them, and re-layouts: 2.75 us -> 0 us
  Pallas kernels: 14.4 us -> 16 us
  blocking collectives: 37.7 us -> 39.2 us
  waiting for transfers between devices: 0.01 us -> 1.24 us
    ppermute x4 -> x3, starting transfers between devices: 6.17 us -> 1.95 us  [on_device(): lax.ppermute(own_filters, 'ch', [(i, i ^ apart) for i in range(4)])]
    unnamed x9 -> x0, local copies, waits for them, and re-layouts: 1.85 us -> none
    all_to_all x1, blocking collectives: 23.2 us -> 24.6 us  [on_device(): data = lax.all_to_all(send, 'ctx', 0, 0, tiled=True)]
    ppermute x4 -> x3, waiting for transfers between devices: 0.01 us -> 1.24 us  [on_device(): lax.ppermute(own_filters, 'ch', [(i, i ^ apart) for i in range(4)])]
    pallas_call x2 -> x3, Pallas kernels: 2.81 us -> 4 us  [the longest x1 2.68 us: on_device(): pl.pallas_call(short_kernel, out_shape=[jax.ShapeDtypeStruct((PARTS, HALF...]
    slice x1 -> x0, local copies, waits for them, and re-layouts: 0.8 us -> none  [on_device(): branches[:, :, TOKENS - LANES:]]
  transfers between devices with their start and end apart: 4 -> 3, of which waited for: 0 -> 1; matrix products, arithmetic and copies ran while one was open for 2% -> 0% of each run, Pallas kernels for 4% -> 5%
where the time goes in v3:
time: 58.6 us; the launch traced here: 58.4 us
  blocking collectives  39.2 us (67%)
  Pallas kernels  16 us (27%)
  starting transfers between devices  1.95 us (3%)
  waiting for transfers between devices  1.24 us (2%)
    all_to_all x1, blocking collectives, on_device(): data = lax.all_to_all(send, 'ctx', 0, 0, tiled=True)  24.6 us
    all_to_all x1, blocking collectives, on_device(): conv = lax.all_to_all(conv, 'ctx', 0, 0, tiled=True)  14.6 us
    pallas_call x1, Pallas kernels, on_device(): pl.pallas_call(conv_kernel, out_shape=jax.ShapeDtypeStruct((PARTS, HALF,...  11 us
    pallas_call x1, Pallas kernels, on_device(): pl.pallas_call(short_kernel, out_shape=[jax.ShapeDtypeStruct((PARTS, HALF...  2.68 us
    ppermute x3, starting transfers between devices, on_device(): lax.ppermute(own_filters, 'ch', [(i, i ^ apart) for i in range(4)])  1.95 us
    pallas_call x1, Pallas kernels, on_device(): pl.pallas_call(prepare_kernel, out_shape=[jax.ShapeDtypeStruct((FILTERS,...  1.28 us
    ppermute x3, waiting for transfers between devices, on_device(): lax.ppermute(own_filters, 'ch', [(i, i ^ apart) for i in range(4)])  1.24 us
  transfers between devices with their start and end apart: 3, of which 1 were waited for; matrix products, arithmetic and copies ran while one was open for 0% of the time, Pallas kernels for 5%

profile of v3, /device:TPU:0, one launch (start us, length us, event | category | flops | bytes accessed | tf_op | source)
XLA Modules:
  0.0 58.4 jit_solution(16910976208154222075)
XLA Ops:
  0.0 1.3 %shard_map.46 = (bf16[16,16,128]{2,1,0:T(8,128)(2,1)S(1)}, f32[3,7,64]{2,1,0:T(8,128)S(1)}, f32[1,64]{1,0:T(1,128)S(1)}, bf16[3,64,2048]{2,1,0:T(8,128)(2,1)S(1)}) custom-call(f32[16,2048]{1,0:T(8,128)} %all_filters_ref.1, f32[3,7,64]{2,1,0:T(8,128)} %bitcast.2, f32[1,64]{1,0:T(1,128)} %bitcast.3, bf16[3,64,2048]{2,1,0:T(8,128)(2,1)} %all_branches_ref.1), custom_call_target="tpu_custom_call" | custom-call | tf_op jit(solution)/shard_map/pallas_call | solution.py:232
  1.3 0.1 collective-permute-start
  1.4 1.7 %collective-permute-start.1 = (bf16[16,16,128]{2,1,0:T(8,128)(2,1)S(1)}, bf16[16,16,128]{2,1,0:T(8,128)(2,1)S(1)}, u32[]{:S(2)}, u32[]{:S(2)}) collective-permute-start(bf16[16,16,128]{2,1,0:T(8,128)(2,1)S(1)} %get-tuple-element.18.own_ref), channel_id=1, source_target_pairs={{0,2},{1,3},{2,0},{3,1},{4,6},{5,7},{6,4},{7,5},{8,10},{9,11},{10,... | collective-permute-start | bytes 196616 | tf_op jit(solution)/shard_map/ppermute | solution.py:250
  3.1 0.1 collective-permute-start.2
  3.2 2.7 %shard_map.47 = (bf16[32,32,128]{2,1,0:T(8,128)(2,1)S(1)}, bf16[32,8,128]{2,1,0:T(8,128)(2,1)S(1)}, f32[64,2048]{1,0:T(8,128)S(1)}, f32[64,2048]{1,0:T(8,128)S(1)}) custom-call(bf16[3,64,2048]{2,1,0:T(8,128)(2,1)S(1)} %get-tuple-element.13.branch_ref, f32[3,7,64]{2,1,0:T(8,128)S(1)} %get-tuple-element.14.taps_ref, f32[1,64]{1,0:T(1,128)S(1)} %get-tuple-element.15.skip_ref), custom_call_target="tpu_custom_call" | custom-call | flops 10000000 | bytes 8388608 | tf_op jit(solution)/shard_map/pallas_call | solution.py:252
  5.9 0.0 collective-permute-done.one_ref
  5.9 0.0 collective-permute-done.1.two_ref
  5.9 1.2 %collective-permute-done.2.three_ref = bf16[16,16,128]{2,1,0:T(8,128)(2,1)S(1)} collective-permute-done((bf16[16,16,128]{2,1,0:T(8,128)(2,1)S(1)}, bf16[16,16,128]{2,1,0:T(8,128)(2,1)S(1)}, u32[]{:S(2)}, u32[]{:S(2)}) %collective-permute-start.2) | collective-permute-done | bytes 65568 | tf_op jit(solution)/shard_map/ppermute | solution.py:250
  7.2 24.6 %all_to_all.10.data_ref = bf16[32,72,128]{2,1,0:T(8,128)(2,1)S(1)} all-to-all(bf16[32,72,128]{2,1,0:T(8,128)(2,1)S(1)} %shard_map.48), channel_id=1, replica_groups=mesh['ctx'=32,'ch'=4] {'ctx'}, dimensions={0} | all-to-all | bytes 1179648 | tf_op jit(solution)/shard_map/all_to_all | solution.py:278
  31.8 11.0 %shard_map.49 = bf16[32,32,128]{2,1,0:T(8,128)(2,1)S(1)} custom-call(bf16[32,72,128]{2,1,0:T(8,128)(2,1)S(1)} %all_to_all.10.data_ref), custom_call_target="tpu_custom_call" | custom-call | tf_op jit(solution)/shard_map/pallas_call | solution.py:279
  42.9 14.6 %all_to_all.11.conv_ref = bf16[32,32,128]{2,1,0:T(8,128)(2,1)S(1)} all-to-all(bf16[32,32,128]{2,1,0:T(8,128)(2,1)S(1)} %shard_map.49), channel_id=1, replica_groups=mesh['ctx'=32,'ch'=4] {'ctx'}, dimensions={0} | all-to-all | bytes 524288 | tf_op jit(solution)/shard_map/all_to_all | solution.py:295
  57.4 1.0 %shard_map.50 = bf16[64,2048]{1,0:T(8,128)(2,1)} custom-call(bf16[32,32,128]{2,1,0:T(8,128)(2,1)S(1)} %all_to_all.11.conv_ref, f32[64,2048]{1,0:T(8,128)S(1)} %get-tuple-element.19.query_ref, f32[64,2048]{1,0:T(8,128)S(1)} %get-tuple-element.20.direct_ref), custom_call_target="tpu_custom_call" | custom-call | tf_op jit(solution)/shard_map/pallas_call | solution.py:296
  (1 shorter events, 0.0 us)
Async XLA Ops:
  1.3 4.6 %collective-permute-start = (bf16[16,16,128]{2,1,0:T(8,128)(2,1)S(1)}, bf16[16,16,128]{2,1,0:T(8,128)(2,1)S(1)}, u32[]{:S(2)}, u32[]{:S(2)}) collective-permute-start(bf16[16,16,128]{2,1,0:T(8,128)(2,1)S(1)} %get-tuple-element.18.own_ref), channel_id=1, source_target_pairs={{0,1},{1,0},{2,3},{3,2},{4,5},{5,4},{6,7},{7,6},{8,9},{9,8},{10,11... | collective-permute-start | bytes 196616 | tf_op jit(solution)/shard_map/ppermute | solution.py:250
  1.4 4.6 %collective-permute-start.1 = (bf16[16,16,128]{2,1,0:T(8,128)(2,1)S(1)}, bf16[16,16,128]{2,1,0:T(8,128)(2,1)S(1)}, u32[]{:S(2)}, u32[]{:S(2)}) collective-permute-start(bf16[16,16,128]{2,1,0:T(8,128)(2,1)S(1)} %get-tuple-element.18.own_ref), channel_id=1, source_target_pairs={{0,2},{1,3},{2,0},{3,1},{4,6},{5,7},{6,4},{7,5},{8,10},{9,11},{10,... | collective-permute-start | bytes 196616 | tf_op jit(solution)/shard_map/ppermute | solution.py:250
  3.1 4.1 %collective-permute-start.2 = (bf16[16,16,128]{2,1,0:T(8,128)(2,1)S(1)}, bf16[16,16,128]{2,1,0:T(8,128)(2,1)S(1)}, u32[]{:S(2)}, u32[]{:S(2)}) collective-permute-start(bf16[16,16,128]{2,1,0:T(8,128)(2,1)S(1)} %get-tuple-element.18.own_ref), channel_id=1, source_target_pairs={{0,3},{1,2},{2,1},{3,0},{4,7},{5,6},{6,5},{7,4},{8,11},{9,10},{10,... | collective-permute-start | bytes 196616 | tf_op jit(solution)/shard_map/ppermute | solution.py:250

commit v4 on v3

--- a/solution.py
+++ b/solution.py
@@ -26,11 +26,10 @@
 
 
 def prepare_kernel(
-    all_filters_ref, all_taps_ref, all_skip_ref, all_branches_ref, cast_ref, taps_ref, skip_ref, branches_ref,
-    filters_ref, rows_ref, semaphores,
+    all_filters_ref, all_taps_ref, all_skip_ref, cast_ref, taps_ref, skip_ref, filters_ref, rows_ref, semaphores
 ):
-    sources = (all_filters_ref, all_taps_ref, all_skip_ref, all_branches_ref)
-    targets = (filters_ref, taps_ref, skip_ref, branches_ref)
+    sources = (all_filters_ref, all_taps_ref, all_skip_ref)
+    targets = (filters_ref, taps_ref, skip_ref)
     copies = [
         pltpu.make_async_copy(source, target, semaphores.at[at])
         for at, (source, target) in enumerate(zip(sources, targets))
@@ -46,8 +45,15 @@
 
 
 def short_kernel(
-    branch_ref, taps_ref, skip_ref, signal_ref, edge_ref, query_ref, direct_ref, rows_ref, edges_ref, small_ref, columns_ref
+    branches_ref, taps_ref, skip_ref, signal_ref, edge_ref, query_ref, direct_ref,
+    branch_ref, semaphores, rows_ref, edges_ref, small_ref, columns_ref,
 ):
+    def fetch(index):
+        rows = pl.ds(pl.multiple_of(index * STEP, STEP), STEP)
+        return pltpu.make_async_copy(branches_ref.at[:, rows, :], branch_ref.at[:, rows, :], semaphores.at[index])
+
+    for index in range(CHANNELS // STEP):
+        fetch(index).start()
     small_ref[...] = jnp.zeros(small_ref.shape, f32)
     for branch in range(3):
         small_ref[8 * branch : 8 * branch + TAPS, :CHANNELS] = taps_ref[branch]
@@ -59,6 +65,7 @@
     def body(index, carry):
         rows = pl.ds(pl.multiple_of(index * STEP, STEP), STEP)
         columns = columns_ref[rows, :]
+        fetch(index).wait()
 
         def column(at):
             return jnp.broadcast_to(columns[:, at : at + 1], (STEP, LANES))
@@ -158,12 +165,14 @@
         signal_ref[opening, :] = jnp.where(first, edges(own)[1], signal_ref[opening, :])
         taps = data_ref[:, HALF + begin : HALF + begin + BLOCKS, :]
         taps_ref[own] = taps.reshape(ROWS, LANES).astype(f32)
+        yield
         for lag in range(0, GROUP, 2):
             near = signal_ref[shift - 2 * lag : shift - 2 * lag + ROWS, :]
             far = signal_ref[shift - 2 * lag - 2 : shift - 2 * lag - 2 + ROWS, :]
             columns = slice(lag * WIDTH, (lag + 2) * WIDTH)
             left_ref[own, 0, :, columns] = jnp.where(low, near, pltpu.roll(far, WIDTH, 1)).astype(bf16)
             left_ref[own, 1, :, columns] = jnp.where(low, pltpu.roll(near, WIDTH, 1), far).astype(bf16)
+            yield
 
     def toeplitz(step, lag, previous):
         own, group = divmod(step, groups)
@@ -194,8 +203,9 @@
         result = signal_ref[shift:, :].astype(bf16).reshape(PARTS, BLOCKS, LANES)
         out_ref[:, own * BLOCKS : (own + 1) * BLOCKS, :] = result
 
-    for own in range(OWN):
-        load(own)
+    for _ in load(0):
+        pass
+    loads = [load(own) for own in range(1, OWN)]
     for lag in range(shift):
         previous = toeplitz(0, lag, previous)
     steps = OWN * groups
@@ -205,6 +215,8 @@
             if step + 1 < steps:
                 for lag in range(half * GROUP, (half + 1) * GROUP):
                     previous = toeplitz(step + 1, lag, previous)
+            if half and own + 1 < OWN:
+                next(loads[own], None)
             product = jnp.dot(
                 left_ref[own, half, : ROWS - shift * group, :], right[step % 2][...], preferred_element_type=f32
             )
@@ -229,23 +241,22 @@
 
 
 def on_device(branches, short_taps, long_filter, skip_gain):
-    own_filters, taps, skip, branches = pl.pallas_call(
+    own_filters, taps, skip = pl.pallas_call(
         prepare_kernel,
         out_shape=[
             jax.ShapeDtypeStruct((FILTERS, BLOCKS, LANES), bf16),
             jax.ShapeDtypeStruct((3, TAPS, CHANNELS), f32),
             jax.ShapeDtypeStruct((1, CHANNELS), f32),
-            jax.ShapeDtypeStruct((3, CHANNELS, TOKENS), bf16),
-        ],
-        in_specs=[pl.BlockSpec(memory_space=pltpu.HBM)] * 4,
-        out_specs=[VMEM] * 4,
+        ],
+        in_specs=[pl.BlockSpec(memory_space=pltpu.HBM)] * 3,
+        out_specs=[VMEM] * 3,
         scratch_shapes=[
             pltpu.VMEM((FILTERS, TOKENS), f32),
             pltpu.VMEM((FILTERS * BLOCKS, LANES), f32),
-            pltpu.SemaphoreType.DMA((4,)),
+            pltpu.SemaphoreType.DMA((3,)),
         ],
         compiler_params=pltpu.CompilerParams(vmem_limit_bytes=8 * 2**20),
-    )(in_hbm(long_filter), in_hbm(short_taps.transpose(0, 2, 1)), in_hbm(skip_gain[None, :]), in_hbm(branches))
+    )(in_hbm(long_filter), in_hbm(short_taps.transpose(0, 2, 1)), in_hbm(skip_gain[None, :]))
     filters = [own_filters] + [
         lax.ppermute(own_filters, "ch", [(i, i ^ apart) for i in range(4)]) for apart in (1, 2, 3)
     ]
@@ -257,9 +268,11 @@
             jax.ShapeDtypeStruct((CHANNELS, TOKENS), f32),
             jax.ShapeDtypeStruct((CHANNELS, TOKENS), f32),
         ],
-        in_specs=[VMEM] * 3,
+        in_specs=[pl.BlockSpec(memory_space=pltpu.HBM), VMEM, VMEM],
         out_specs=[VMEM] * 4,
         scratch_shapes=[
+            pltpu.VMEM((3, CHANNELS, TOKENS), bf16),
+            pltpu.SemaphoreType.DMA((CHANNELS // STEP,)),
             pltpu.VMEM((CHANNELS * BLOCKS, LANES), f32),
             pltpu.VMEM((3, CHANNELS, LANES), f32),
             pltpu.VMEM((LANES, LANES), f32),
@@ -267,7 +280,7 @@
         ],
         compiler_params=pltpu.CompilerParams(vmem_limit_bytes=16 * 2**20),
         cost_estimate=pl.CostEstimate(flops=10**7, bytes_accessed=8 * 2**20, transcendentals=0),
-    )(branches, taps, skip)
+    )(in_hbm(branches), taps, skip)
     send = pl.pallas_call(
         pack_kernel,
         out_shape=jax.ShapeDtypeStruct((PARTS, 2 * HALF + EDGE, LANES), bf16),

time: 58.6 us -> 58.2 us (level)
  waiting for transfers between devices: 1.24 us -> 0.41 us
    pallas_call x1, Pallas kernels: 2.68 us -> 3.52 us  [on_device(): pl.pallas_call(short_kernel, out_shape=[jax.ShapeDtypeStruct((PARTS, HALF...]
    ppermute x3, waiting for transfers between devices: 1.24 us -> 0.41 us  [on_device(): lax.ppermute(own_filters, 'ch', [(i, i ^ apart) for i in range(4)])]
  transfers between devices with their start and end apart: 3 -> 3, of which waited for: 1 -> 1; matrix products, arithmetic and copies ran while one was open for 0% -> 0% of each run, Pallas kernels for 5% -> 6%
where the time goes in v4:
time: 58.2 us; the launch traced here: 58 us
  blocking collectives  39.2 us (67%)
  Pallas kernels  16.4 us (28%)
  starting transfers between devices  1.94 us (3%)
    all_to_all x1, blocking collectives, on_device(): data = lax.all_to_all(send, 'ctx', 0, 0, tiled=True)  24.7 us
    all_to_all x1, blocking collectives, on_device(): conv = lax.all_to_all(conv, 'ctx', 0, 0, tiled=True)  14.6 us
    pallas_call x1, Pallas kernels, on_device(): pl.pallas_call(conv_kernel, out_shape=jax.ShapeDtypeStruct((PARTS, HALF,...  10.9 us
    pallas_call x1, Pallas kernels, on_device(): pl.pallas_call(short_kernel, out_shape=[jax.ShapeDtypeStruct((PARTS, HALF...  3.52 us
    ppermute x3, starting transfers between devices, on_device(): lax.ppermute(own_filters, 'ch', [(i, i ^ apart) for i in range(4)])  1.94 us
  transfers between devices with their start and end apart: 3, of which 1 were waited for; matrix products, arithmetic and copies ran while one was open for 0% of the time, Pallas kernels for 6%

profile of v4, /device:TPU:0, one launch (start us, length us, event | category | flops | bytes accessed | tf_op | source)
XLA Modules:
  0.0 58.0 jit_solution(7707908105810297482)
XLA Ops:
  0.0 1.0 %shard_map.46 = (bf16[16,16,128]{2,1,0:T(8,128)(2,1)S(1)}, f32[3,7,64]{2,1,0:T(8,128)S(1)}, f32[1,64]{1,0:T(1,128)S(1)}) custom-call(f32[16,2048]{1,0:T(8,128)} %all_filters_ref.1, f32[3,7,64]{2,1,0:T(8,128)} %bitcast.2, f32[1,64]{1,0:T(1,128)} %bitcast.3), custom_call_target="tpu_custom_call" | custom-call | tf_op jit(solution)/shard_map/pallas_call | solution.py:244
  1.0 1.2 %collective-permute-start.2 = (bf16[16,16,128]{2,1,0:T(8,128)(2,1)S(1)}, bf16[16,16,128]{2,1,0:T(8,128)(2,1)S(1)}, u32[]{:S(2)}, u32[]{:S(2)}) collective-permute-start(bf16[16,16,128]{2,1,0:T(8,128)(2,1)S(1)} %get-tuple-element.16.own_ref), channel_id=1, source_target_pairs={{0,3},{1,2},{2,1},{3,0},{4,7},{5,6},{6,5},{7,4},{8,11},{9,10},{10,... | collective-permute-start | bytes 196616 | tf_op jit(solution)/shard_map/ppermute | solution.py:261
  2.2 0.7 %collective-permute-start.1 = (bf16[16,16,128]{2,1,0:T(8,128)(2,1)S(1)}, bf16[16,16,128]{2,1,0:T(8,128)(2,1)S(1)}, u32[]{:S(2)}, u32[]{:S(2)}) collective-permute-start(bf16[16,16,128]{2,1,0:T(8,128)(2,1)S(1)} %get-tuple-element.16.own_ref), channel_id=1, source_target_pairs={{0,2},{1,3},{2,0},{3,1},{4,6},{5,7},{6,4},{7,5},{8,10},{9,11},{10,... | collective-permute-start | bytes 196616 | tf_op jit(solution)/shard_map/ppermute | solution.py:261
  2.8 0.1 collective-permute-start
  2.9 3.5 %shard_map.47 = (bf16[32,32,128]{2,1,0:T(8,128)(2,1)S(1)}, bf16[32,8,128]{2,1,0:T(8,128)(2,1)S(1)}, f32[64,2048]{1,0:T(8,128)S(1)}, f32[64,2048]{1,0:T(8,128)S(1)}) custom-call(bf16[3,64,2048]{2,1,0:T(8,128)(2,1)} %branches_ref.1, f32[3,7,64]{2,1,0:T(8,128)S(1)} %get-tuple-element.12.taps_ref, f32[1,64]{1,0:T(1,128)S(1)} %get-tuple-element.13.skip_ref), custom_call_target="tpu_custom_call" | custom-call | flops 10000000 | bytes 8388608 | tf_op jit(solution)/shard_map/pallas_call | solution.py:263
  6.5 0.0 collective-permute-done.2.three_ref
  6.5 0.4 collective-permute-done.1.two_ref
  6.9 0.0 collective-permute-done.one_ref
  6.9 24.7 %all_to_all.10.data_ref = bf16[32,72,128]{2,1,0:T(8,128)(2,1)S(1)} all-to-all(bf16[32,72,128]{2,1,0:T(8,128)(2,1)S(1)} %shard_map.48), channel_id=1, replica_groups=mesh['ctx'=32,'ch'=4] {'ctx'}, dimensions={0} | all-to-all | bytes 1179648 | tf_op jit(solution)/shard_map/all_to_all | solution.py:291
  31.6 10.9 %shard_map.49 = bf16[32,32,128]{2,1,0:T(8,128)(2,1)S(1)} custom-call(bf16[32,72,128]{2,1,0:T(8,128)(2,1)S(1)} %all_to_all.10.data_ref), custom_call_target="tpu_custom_call" | custom-call | tf_op jit(solution)/shard_map/pallas_call | solution.py:292
  42.5 14.6 %all_to_all.11.conv_ref = bf16[32,32,128]{2,1,0:T(8,128)(2,1)S(1)} all-to-all(bf16[32,32,128]{2,1,0:T(8,128)(2,1)S(1)} %shard_map.49), channel_id=1, replica_groups=mesh['ctx'=32,'ch'=4] {'ctx'}, dimensions={0} | all-to-all | bytes 524288 | tf_op jit(solution)/shard_map/all_to_all | solution.py:308
  57.0 1.0 %shard_map.50 = bf16[64,2048]{1,0:T(8,128)(2,1)} custom-call(bf16[32,32,128]{2,1,0:T(8,128)(2,1)S(1)} %all_to_all.11.conv_ref, f32[64,2048]{1,0:T(8,128)S(1)} %get-tuple-element.17.query_ref, f32[64,2048]{1,0:T(8,128)S(1)} %get-tuple-element.18.direct_ref), custom_call_target="tpu_custom_call" | custom-call | tf_op jit(solution)/shard_map/pallas_call | solution.py:309
  (1 shorter events, 0.0 us)
Async XLA Ops:
  1.0 5.5 %collective-permute-start.2 = (bf16[16,16,128]{2,1,0:T(8,128)(2,1)S(1)}, bf16[16,16,128]{2,1,0:T(8,128)(2,1)S(1)}, u32[]{:S(2)}, u32[]{:S(2)}) collective-permute-start(bf16[16,16,128]{2,1,0:T(8,128)(2,1)S(1)} %get-tuple-element.16.own_ref), channel_id=1, source_target_pairs={{0,3},{1,2},{2,1},{3,0},{4,7},{5,6},{6,5},{7,4},{8,11},{9,10},{10,... | collective-permute-start | bytes 196616 | tf_op jit(solution)/shard_map/ppermute | solution.py:261
  2.2 4.7 %collective-permute-start.1 = (bf16[16,16,128]{2,1,0:T(8,128)(2,1)S(1)}, bf16[16,16,128]{2,1,0:T(8,128)(2,1)S(1)}, u32[]{:S(2)}, u32[]{:S(2)}) collective-permute-start(bf16[16,16,128]{2,1,0:T(8,128)(2,1)S(1)} %get-tuple-element.16.own_ref), channel_id=1, source_target_pairs={{0,2},{1,3},{2,0},{3,1},{4,6},{5,7},{6,4},{7,5},{8,10},{9,11},{10,... | collective-permute-start | bytes 196616 | tf_op jit(solution)/shard_map/ppermute | solution.py:261
  2.8 4.0 %collective-permute-start = (bf16[16,16,128]{2,1,0:T(8,128)(2,1)S(1)}, bf16[16,16,128]{2,1,0:T(8,128)(2,1)S(1)}, u32[]{:S(2)}, u32[]{:S(2)}) collective-permute-start(bf16[16,16,128]{2,1,0:T(8,128)(2,1)S(1)} %get-tuple-element.16.own_ref), channel_id=1, source_target_pairs={{0,1},{1,0},{2,3},{3,2},{4,5},{5,4},{6,7},{7,6},{8,9},{9,8},{10,11... | collective-permute-start | bytes 196616 | tf_op jit(solution)/shard_map/ppermute | solution.py:261

commit v5 on v3

v5 whole, which is shorter than its diff:
```python
import jax
import jax.numpy as jnp
from jax import lax
from jax.experimental import pallas as pl
from jax.experimental.pallas import tpu as pltpu
from jax.sharding import PartitionSpec as P

f32, bf16 = jnp.float32, jnp.bfloat16
LANES = 128
TAPS = 7
REACH = TAPS - 1
CHANNELS = 64
TOKENS = 2048
BLOCKS = TOKENS // LANES
PARTS = 32
FILTERS = 16
OWN = CHANNELS // PARTS
ROWS = PARTS * BLOCKS
HALF = OWN * BLOCKS
EDGES_AT = HALF + BLOCKS
EDGE = 8
LOW, SKIP = 48, 96
STEP = 16
GROUP = 8
WIDTH = LANES // 2
VMEM = pl.BlockSpec(memory_space=pltpu.VMEM)


def prepare_kernel(
    all_filters_ref, all_taps_ref, all_skip_ref, all_branches_ref, same_ref, other_ref, taps_ref, skip_ref, branches_ref,
    filters_ref, rows_ref, semaphores,
):
    sources = (all_filters_ref, all_taps_ref, all_skip_ref, all_branches_ref)
    targets = (filters_ref, taps_ref, skip_ref, branches_ref)
    copies = [
        pltpu.make_async_copy(source, target, semaphores.at[at])
        for at, (source, target) in enumerate(zip(sources, targets))
    ]
    for copy in copies:
        copy.start()
    copies[0].wait()
    for block in range(BLOCKS):
        rows_ref[pl.ds(block, FILTERS, stride=BLOCKS), :] = filters_ref[:, block * LANES : (block + 1) * LANES]
    rows = rows_ref[...].reshape(FILTERS // 2, 2, BLOCKS, LANES)
    second = lax.rem(lax.axis_index("ch"), 2) == 1
    same_ref[...] = jnp.where(second, rows[:, 1], rows[:, 0]).astype(bf16)
    other_ref[...] = jnp.where(second, rows[:, 0], rows[:, 1]).astype(bf16)
    for copy in copies[1:]:
        copy.wait()


def stand(columns_ref, small_ref, taps_ref, skip_ref):
    small_ref[...] = jnp.zeros(small_ref.shape, f32)
    for branch in range(3):
        small_ref[8 * branch : 8 * branch + TAPS, :CHANNELS] = taps_ref[branch]
    small_ref[24:25, :CHANNELS] = skip_ref[...]
    columns_ref[...] = small_ref[...].T


def filtered(branch_ref, columns, branch, rows):
    lane = lax.broadcasted_iota(jnp.int32, (STEP, LANES), 1)
    taps = [jnp.broadcast_to(columns[:, 8 * branch + tap : 8 * branch + tap + 1], (STEP, LANES)) for tap in range(TAPS)]
    before = [jnp.zeros((STEP, LANES), f32)] * REACH
    for block in range(BLOCKS):
        own = branch_ref[branch, rows, block * LANES : (block + 1) * LANES].astype(f32)
        total = taps[0] * own
        for tap in range(1, TAPS):
            turned = pltpu.roll(own, tap, 1)
            total += taps[tap] * jnp.where(lane < tap, before[tap - 1], turned)
            before[tap - 1] = turned
        yield total


def short_kernel(
    branch_ref, taps_ref, skip_ref, signal_ref, edge_ref, query_ref, direct_ref, rows_ref, edges_ref, small_ref, columns_ref
):
    stand(columns_ref, small_ref, taps_ref, skip_ref)
    first = lax.broadcasted_iota(jnp.int32, (STEP, LANES), 1) < REACH

    def body(index, carry):
        rows = pl.ds(pl.multiple_of(index * STEP, STEP), STEP)
        columns = columns_ref[rows, :]
        skip = jnp.broadcast_to(columns[:, 24:25], (STEP, LANES))
        for block, total in enumerate(filtered(branch_ref, columns, 1, rows)):
            direct_ref[rows, block * LANES : (block + 1) * LANES] = total
            if block == 0:
                edges_ref[1, rows, :] = total
        for block, total in enumerate(filtered(branch_ref, columns, 2, rows)):
            at = slice(block * LANES, (block + 1) * LANES)
            gated = direct_ref[rows, at] * total
            direct_ref[rows, at] = skip * gated
            rows_ref[pl.ds(index * (STEP * BLOCKS) + block, STEP, stride=BLOCKS), :] = gated
            if block == 0:
                edges_ref[2, rows, :] = total
        for block, total in enumerate(filtered(branch_ref, columns, 0, rows)):
            at = slice(block * LANES, (block + 1) * LANES)
            direct = total * direct_ref[rows, at]
            query_ref[rows, at] = total if block else jnp.where(first, 1.0, total)
            direct_ref[rows, at] = direct if block else jnp.where(first, 0.0, direct)
            if block == 0:
                edges_ref[0, rows, :] = total
        return carry

    lax.fori_loop(0, CHANNELS // STEP, body, 0)
    signal_ref[...] = rows_ref[...].reshape(PARTS, HALF, LANES).astype(bf16)
    lane = lax.broadcasted_iota(jnp.int32, (CHANNELS, LANES), 1)
    edge = jnp.where(lane < REACH, edges_ref[0], 0.0)
    for branch in range(3):
        if branch:
            edge += pltpu.roll(jnp.where(lane < REACH, edges_ref[branch], 0.0), 8 * branch, 1)
        place = 24 + 8 * branch
        last = branch_ref[branch, :, TOKENS - LANES :].astype(f32)
        for tap in range(1, TAPS):
            weight = columns_ref[:CHANNELS, 8 * branch + tap : 8 * branch + tap + 1]
            share = weight * pltpu.roll(last, place + tap, 1)
            edge += jnp.where((lane >= place) & (lane < place + tap), share, 0.0)
    skip = columns_ref[:CHANNELS, 24:25]
    high = edge.astype(bf16).astype(f32)
    skip_high = skip.astype(bf16).astype(f32)
    gains = jnp.where(lane < SKIP, 0.0, jnp.where(lane < SKIP + 8, skip_high, skip - skip_high))
    edges_ref[0] = high + pltpu.roll(edge - high, LOW, 1) + gains
    rows_ref[: PARTS * EDGE, :] = jnp.zeros((PARTS * EDGE, LANES), f32)
    for own in range(OWN):
        rows_ref[pl.ds(own, PARTS, stride=EDGE), :] = edges_ref[0, pl.ds(own, PARTS, stride=OWN), :]
    edge_ref[...] = rows_ref[: PARTS * EDGE, :].reshape(PARTS, EDGE, LANES).astype(bf16)


def pack_kernel(signal_ref, edge_ref, own_ref, one_ref, two_ref, three_ref, send_ref):
    send_ref[:, :HALF, :] = signal_ref[...]
    send_ref[:, EDGES_AT:, :] = edge_ref[...]
    here = lax.axis_index("ch")
    owned = FILTERS // OWN
    for apart, taps_from in enumerate((own_ref, one_ref, two_ref, three_ref)):
        begin = pl.multiple_of((here ^ apart) * owned, owned)
        send_ref[pl.ds(begin, owned), HALF:EDGES_AT, :] = taps_from[...]


def conv_kernel(data_ref, *rest):
    *inputs, out_ref, signal_ref, taps_ref, edge_ref, left_ref, even_ref, odd_ref, sum_ref = rest
    core = lax.rem(lax.axis_index("ch"), 2)
    channel = 1 - core if inputs else core
    shift = 2 * GROUP
    groups = ROWS // shift
    row = lax.broadcasted_iota(jnp.int32, (WIDTH, LANES), 0)
    lane = lax.broadcasted_iota(jnp.int32, (WIDTH, LANES), 1)
    above = lane >= row
    low = lax.broadcasted_iota(jnp.int32, (ROWS, LANES), 1) < WIDTH
    right = (even_ref, odd_ref)
    previous = jnp.zeros((WIDTH, LANES), bf16)
    first = lax.broadcasted_iota(jnp.int32, (PARTS, LANES), 1) < REACH
    start = lax.broadcasted_iota(jnp.int32, (PARTS, LANES), 0) == 0
    edge_ref[...] = data_ref[:, EDGES_AT:, :].reshape(PARTS * EDGE, LANES).astype(f32)
    opening = pl.ds(shift, PARTS, stride=BLOCKS)

    def turn_back(value, by):
        return pltpu.roll(value, LANES - by, 1)

    def place(at):
        return pl.ds(pl.multiple_of(at * BLOCKS, BLOCKS), BLOCKS)

    def edges():
        rows = [edge_ref[pl.ds(at, PARTS, stride=EDGE), :] for at in range(OWN)]
        row = jnp.where(channel == 1, rows[1], rows[0])
        share = row + turn_back(row, LOW)
        other = jnp.where(start, 0.0, pltpu.roll(turn_back(share, 24), 1, 0))
        short = share + other
        gain = turn_back(row, SKIP) + turn_back(row, SKIP + 8)
        return short, turn_back(short, 8) * turn_back(short, 16), gain

    signal_ref[:shift, :] = jnp.zeros((shift, LANES), f32)
    signal_ref[shift:, :] = data_ref[:, place(channel), :].reshape(ROWS, LANES).astype(f32)
    signal_ref[opening, :] = jnp.where(first, edges()[1], signal_ref[opening, :])
    taps = inputs[0][...] if inputs else data_ref[:, HALF:EDGES_AT, :]
    taps_ref[...] = taps.reshape(ROWS, LANES).astype(f32)
    for lag in range(0, GROUP, 2):
        near = signal_ref[shift - 2 * lag : shift - 2 * lag + ROWS, :]
        far = signal_ref[shift - 2 * lag - 2 : shift - 2 * lag - 2 + ROWS, :]
        columns = slice(lag * WIDTH, (lag + 2) * WIDTH)
        left_ref[0, :, columns] = jnp.where(low, near, pltpu.roll(far, WIDTH, 1)).astype(bf16)
        left_ref[1, :, columns] = jnp.where(low, pltpu.roll(near, WIDTH, 1), far).astype(bf16)

    def toeplitz(group, lag, previous):
        block = group * shift + lag
        current = jnp.broadcast_to(taps_ref[block : block + 1, :], (WIDTH, LANES))
        current = pltpu.roll(current, 0, 1, stride=1, stride_axis=0).astype(bf16)
        right[group % 2][
            (lag // 2) * WIDTH : (lag // 2 + 1) * WIDTH, (lag % 2) * LANES : (lag % 2 + 1) * LANES
        ] = jnp.where(above, current, previous)
        return current

    for lag in range(shift):
        previous = toeplitz(0, lag, previous)
    for group in range(groups):
        for half in range(2):
            if group + 1 < groups:
                for lag in range(half * GROUP, (half + 1) * GROUP):
                    previous = toeplitz(group + 1, lag, previous)
            product = jnp.dot(
                left_ref[half, : ROWS - shift * group, :], right[group % 2][...], preferred_element_type=f32
            )
            if group == 0:
                sum_ref[half, shift:, :] = product
            else:
                sum_ref[half, shift + shift * group :, :] += product

    for half in range(2):
        sum_ref[half, :shift, :] = jnp.zeros((shift, 2 * LANES), f32)

    def gather(half, back):
        here, there = shift - back, shift - back - 1
        return sum_ref[half, here : here + ROWS, :LANES] + sum_ref[half, there : there + ROWS, LANES:]

    turned = jnp.where(low, pltpu.roll(gather(1, 1), WIDTH, 1), pltpu.roll(gather(1, 0), WIDTH, 1))
    signal_ref[shift:, :] = gather(0, 0) + turned
    query, gated, gain = edges()
    conv = signal_ref[opening, :]
    signal_ref[opening, :] = jnp.where(first, query * (conv + gain * gated), conv)
    result = signal_ref[shift:, :].astype(bf16).reshape(PARTS, BLOCKS, LANES)
    if inputs:
        out_ref[:, place(channel), :] = result
        out_ref[:, place(1 - channel), :] = inputs[1][...]
    else:
        out_ref[...] = result


def convolve(data, *inputs):
    return pl.pallas_call(
        conv_kernel,
        out_shape=jax.ShapeDtypeStruct((PARTS, HALF if inputs else BLOCKS, LANES), bf16),
        in_specs=[VMEM] * (1 + len(inputs)),
        out_specs=VMEM,
        scratch_shapes=[
            pltpu.VMEM((2 * GROUP + ROWS, LANES), f32),
            pltpu.VMEM((ROWS, LANES), f32),
            pltpu.VMEM((PARTS * EDGE, LANES), f32),
            pltpu.VMEM((2, ROWS, GROUP * WIDTH), bf16),
            pltpu.VMEM((GROUP * WIDTH, 2 * LANES), bf16),
            pltpu.VMEM((GROUP * WIDTH, 2 * LANES), bf16),
            pltpu.VMEM((2, 2 * GROUP + ROWS, 2 * LANES), f32),
        ],
        compiler_params=pltpu.CompilerParams(vmem_limit_bytes=16 * 2**20),
        cost_estimate=pl.CostEstimate(flops=4 * 10**9, bytes_accessed=2**20, transcendentals=0),
    )(data, *inputs)


def mix_kernel(conv_ref, query_ref, direct_ref, out_ref, rows_ref):
    rows_ref[...] = conv_ref[...].reshape(CHANNELS * BLOCKS, LANES).astype(f32)
    for block in range(BLOCKS):
        at = slice(block * LANES, (block + 1) * LANES)
        conv = rows_ref[pl.ds(block, CHANNELS, stride=BLOCKS), :]
        out_ref[:, at] = (query_ref[:, at] * conv + direct_ref[:, at]).astype(bf16)


def in_hbm(array):
    return pltpu.with_memory_space_constraint(array, pltpu.HBM)


def on_device(branches, short_taps, long_filter, skip_gain):
    same, other, taps, skip, branches = pl.pallas_call(
        prepare_kernel,
        out_shape=[
            jax.ShapeDtypeStruct((FILTERS // 2, BLOCKS, LANES), bf16),
            jax.ShapeDtypeStruct((FILTERS // 2, BLOCKS, LANES), bf16),
            jax.ShapeDtypeStruct((3, TAPS, CHANNELS), f32),
            jax.ShapeDtypeStruct((1, CHANNELS), f32),
            jax.ShapeDtypeStruct((3, CHANNELS, TOKENS), bf16),
        ],
        in_specs=[pl.BlockSpec(memory_space=pltpu.HBM)] * 4,
        out_specs=[VMEM] * 5,
        scratch_shapes=[
            pltpu.VMEM((FILTERS, TOKENS), f32),
            pltpu.VMEM((FILTERS * BLOCKS, LANES), f32),
            pltpu.SemaphoreType.DMA((4,)),
        ],
        compiler_params=pltpu.CompilerParams(vmem_limit_bytes=8 * 2**20),
    )(in_hbm(long_filter), in_hbm(short_taps.transpose(0, 2, 1)), in_hbm(skip_gain[None, :]), in_hbm(branches))
    filters = [same] + [
        lax.ppermute(sent, "ch", [(i, i ^ apart) for i in range(4)]) for apart, sent in ((1, other), (2, same), (3, other))
    ]
    signal, edge, query, direct = pl.pallas_call(
        short_kernel,
        out_shape=[
            jax.ShapeDtypeStruct((PARTS, HALF, LANES), bf16),
            jax.ShapeDtypeStruct((PARTS, EDGE, LANES), bf16),
            jax.ShapeDtypeStruct((CHANNELS, TOKENS), f32),
            jax.ShapeDtypeStruct((CHANNELS, TOKENS), f32),
        ],
        in_specs=[VMEM] * 3,
        out_specs=[VMEM] * 4,
        scratch_shapes=[
            pltpu.VMEM((CHANNELS * BLOCKS, LANES), f32),
            pltpu.VMEM((3, CHANNELS, LANES), f32),
            pltpu.VMEM((LANES, LANES), f32),
            pltpu.VMEM((LANES, LANES), f32),
        ],
        compiler_params=pltpu.CompilerParams(vmem_limit_bytes=16 * 2**20),
        cost_estimate=pl.CostEstimate(flops=10**7, bytes_accessed=8 * 2**20, transcendentals=0),
    )(branches, taps, skip)
    send = pl.pallas_call(
        pack_kernel,
        out_shape=jax.ShapeDtypeStruct((PARTS, EDGES_AT + EDGE, LANES), bf16),
        in_specs=[VMEM] * 6,
        out_specs=VMEM,
        compiler_params=pltpu.CompilerParams(vmem_limit_bytes=16 * 2**20),
    )(signal, edge, *filters)
    data = lax.all_to_all(send, "ctx", 0, 0, tiled=True)
    swapped = lax.ppermute(data[:, HALF:EDGES_AT, :], "ch", [(i, i ^ 1) for i in range(4)])
    conv = convolve(data, swapped, convolve(data))
    conv = lax.all_to_all(conv, "ctx", 0, 0, tiled=True)
    return pl.pallas_call(
        mix_kernel,
        out_shape=jax.ShapeDtypeStruct((CHANNELS, TOKENS), bf16),
        in_specs=[VMEM] * 3,
        out_specs=VMEM,
        scratch_shapes=[pltpu.VMEM((CHANNELS * BLOCKS, LANES), f32)],
        compiler_params=pltpu.CompilerParams(vmem_limit_bytes=32 * 2**20),
    )(conv, query, direct)


def solution(mesh):
    placed = (P(None, "ch", "ctx"), P(None, "ch", None), P("ch", "ctx"), P("ch"))
    return jax.shard_map(
        on_device, mesh=mesh, in_specs=placed, out_specs=P("ch", "ctx"), check_vma=False
    )
```

time: 58.6 us -> 57.2 us (0.976)
  blocking collectives: 39.2 us -> 38.3 us
  waiting for transfers between devices: 1.24 us -> 0.54 us
    all_to_all x1, blocking collectives: 24.6 us -> 23.2 us  [on_device(): data = lax.all_to_all(send, 'ctx', 0, 0, tiled=True)]
    ppermute x3 -> x4, waiting for transfers between devices: 1.24 us -> 0.54 us  [the longest x3 0.54 us: on_device(): lax.ppermute(sent, 'ch', [(i, i ^ apart) for i in range(4)])]
    ppermute x3 -> x4, starting transfers between devices: 1.95 us -> 2.21 us  [the longest x3 1.95 us: on_device(): lax.ppermute(sent, 'ch', [(i, i ^ apart) for i in range(4)])]
    pallas_call x3 -> x4, Pallas kernels: 12.3 us -> 12.2 us  [the longest x2 10.9 us: convolve(): pl.pallas_call(conv_kernel, out_shape=jax.ShapeDtypeStruct((PARTS, HALF i...]
  transfers between devices with their start and end apart: 3 -> 4, of which waited for: 1 -> 1; matrix products, arithmetic and copies ran while one was open for 0% -> 0% of each run, Pallas kernels for 5% -> 14%
where the time goes in v5:
time: 57.2 us; the launch traced here: 57 us
  blocking collectives  38.3 us (67%)
  Pallas kernels  15.9 us (28%)
  starting transfers between devices  2.21 us (4%)
    all_to_all x1, blocking collectives, on_device(): data = lax.all_to_all(send, 'ctx', 0, 0, tiled=True)  23.2 us
    all_to_all x1, blocking collectives, on_device(): conv = lax.all_to_all(conv, 'ctx', 0, 0, tiled=True)  15.1 us
    pallas_call x2, Pallas kernels, convolve(): pl.pallas_call(conv_kernel, out_shape=jax.ShapeDtypeStruct((PARTS, HALF i...  10.9 us
    pallas_call x1, Pallas kernels, on_device(): pl.pallas_call(short_kernel, out_shape=[jax.ShapeDtypeStruct((PARTS, HALF...  2.68 us
    ppermute x3, starting transfers between devices, on_device(): lax.ppermute(sent, 'ch', [(i, i ^ apart) for i in range(4)])  1.95 us
    pallas_call x1, Pallas kernels, on_device(): pl.pallas_call(prepare_kernel, out_shape=[jax.ShapeDtypeStruct((FILTERS /...  1.28 us
  transfers between devices with their start and end apart: 4, of which 1 were waited for; matrix products, arithmetic and copies ran while one was open for 0% of the time, Pallas kernels for 14%

profile of v5, /device:TPU:0, one launch (start us, length us, event | category | flops | bytes accessed | tf_op | source)
XLA Modules:
  0.0 57.0 jit_solution(4340271482992014620)
XLA Ops:
  0.0 1.3 %shard_map.46 = (bf16[8,16,128]{2,1,0:T(8,128)(2,1)S(1)}, bf16[8,16,128]{2,1,0:T(8,128)(2,1)S(1)}, f32[3,7,64]{2,1,0:T(8,128)S(1)}, f32[1,64]{1,0:T(1,128)S(1)}, bf16[3,64,2048]{2,1,0:T(8,128)(2,1)S(1)}) custom-call(f32[16,2048]{1,0:T(8,128)} %all_filters_ref.1, f32[3,7,64]{2,1,0:T(8,128)} %bitcast.2, f32[1,64]{1,0:T(1,128)} %bitcast.3, ...), custom_call_target="tpu_custom_call" | custom-call | tf_op jit(solution)/shard_map/pallas_call | solution.py:259
  1.3 0.1 collective-permute-start
  1.4 1.7 %collective-permute-start.1 = (bf16[8,16,128]{2,1,0:T(8,128)(2,1)S(1)}, bf16[8,16,128]{2,1,0:T(8,128)(2,1)S(1)}, u32[]{:S(2)}, u32[]{:S(2)}) collective-permute-start(bf16[8,16,128]{2,1,0:T(8,128)(2,1)S(1)} %get-tuple-element.19.own_ref), channel_id=1, source_target_pairs={{0,2},{1,3},{2,0},{3,1},{4,6},{5,7},{6,4},{7,5},{8,10},{9,11},{10,... | collective-permute-start | bytes 98312 | tf_op jit(solution)/shard_map/ppermute | solution.py:278
  3.1 0.1 collective-permute-start.2
  3.2 2.7 %shard_map.47 = (bf16[32,32,128]{2,1,0:T(8,128)(2,1)S(1)}, bf16[32,8,128]{2,1,0:T(8,128)(2,1)S(1)}, f32[64,2048]{1,0:T(8,128)S(1)}, f32[64,2048]{1,0:T(8,128)S(1)}) custom-call(bf16[3,64,2048]{2,1,0:T(8,128)(2,1)S(1)} %get-tuple-element.14.branch_ref, f32[3,7,64]{2,1,0:T(8,128)S(1)} %get-tuple-element.15.taps_ref, f32[1,64]{1,0:T(1,128)S(1)} %get-tuple-element.16.skip_ref), custom_call_target="tpu_custom_call" | custom-call | flops 10000000 | bytes 8388608 | tf_op jit(solution)/shard_map/pallas_call | solution.py:280
  5.9 0.0 collective-permute-done.one_ref
  5.9 0.0 collective-permute-done.1.two_ref
  5.9 0.5 collective-permute-done.2.three_ref
  6.5 23.2 %all_to_all.10.data_ref = bf16[32,56,128]{2,1,0:T(8,128)(2,1)S(1)} all-to-all(bf16[32,56,128]{2,1,0:T(8,128)(2,1)S(1)} %shard_map.48), channel_id=1, replica_groups=mesh['ctx'=32,'ch'=4] {'ctx'}, dimensions={0} | all-to-all | bytes 917504 | tf_op jit(solution)/shard_map/all_to_all | solution.py:306
  29.8 0.3 collective-permute-start.3
  30.0 5.4 %shard_map.49.rest_1_ = bf16[32,16,128]{2,1,0:T(8,128)(2,1)S(1)} custom-call(bf16[32,56,128]{2,1,0:T(8,128)(2,1)S(1)} %all_to_all.10.data_ref), custom_call_target="tpu_custom_call" | custom-call | flops 4000000000 | bytes 1048576 | tf_op jit(solution)/shard_map/pallas_call | solution.py:227
  35.5 0.0 collective-permute-done.3.rest_0_
  35.5 5.4 %shard_map.50 = bf16[32,32,128]{2,1,0:T(8,128)(2,1)S(1)} custom-call(bf16[32,56,128]{2,1,0:T(8,128)(2,1)S(1)} %all_to_all.10.data_ref, bf16[32,16,128]{2,1,0:T(8,128)(2,1)S(1)} %collective-permute-done.3.rest_0_, bf16[32,16,128]{2,1,0:T(8,128)(2,1)S(1)} %shard_map.49.rest_1_), custom_call_target="tpu_custom_call" | custom-call | flops 4000000000 | bytes 1048576 | tf_op jit(solution)/shard_map/pallas_call | solution.py:227
  40.9 15.1 %all_to_all.11.conv_ref = bf16[32,32,128]{2,1,0:T(8,128)(2,1)S(1)} all-to-all(bf16[32,32,128]{2,1,0:T(8,128)(2,1)S(1)} %shard_map.50), channel_id=1, replica_groups=mesh['ctx'=32,'ch'=4] {'ctx'}, dimensions={0} | all-to-all | bytes 524288 | tf_op jit(solution)/shard_map/all_to_all | solution.py:309
  56.0 1.0 %shard_map.51 = bf16[64,2048]{1,0:T(8,128)(2,1)} custom-call(bf16[32,32,128]{2,1,0:T(8,128)(2,1)S(1)} %all_to_all.11.conv_ref, f32[64,2048]{1,0:T(8,128)S(1)} %get-tuple-element.21.query_ref, f32[64,2048]{1,0:T(8,128)S(1)} %get-tuple-element.22.direct_ref), custom_call_target="tpu_custom_call" | custom-call | tf_op jit(solution)/shard_map/pallas_call | solution.py:310
  (2 shorter events, 0.0 us)
Async XLA Ops:
  1.3 4.6 %collective-permute-start = (bf16[8,16,128]{2,1,0:T(8,128)(2,1)S(1)}, bf16[8,16,128]{2,1,0:T(8,128)(2,1)S(1)}, u32[]{:S(2)}, u32[]{:S(2)}) collective-permute-start(bf16[8,16,128]{2,1,0:T(8,128)(2,1)S(1)} %get-tuple-element.20), channel_id=1, source_target_pairs={{0,1},{1,0},{2,3},{3,2},{4,5},{5,4},{6,7},{7,6},{8,9},{9,8},{10,11... | collective-permute-start | bytes 98312 | tf_op jit(solution)/shard_map/ppermute | solution.py:278
  1.4 4.6 %collective-permute-start.1 = (bf16[8,16,128]{2,1,0:T(8,128)(2,1)S(1)}, bf16[8,16,128]{2,1,0:T(8,128)(2,1)S(1)}, u32[]{:S(2)}, u32[]{:S(2)}) collective-permute-start(bf16[8,16,128]{2,1,0:T(8,128)(2,1)S(1)} %get-tuple-element.19.own_ref), channel_id=1, source_target_pairs={{0,2},{1,3},{2,0},{3,1},{4,6},{5,7},{6,4},{7,5},{8,10},{9,11},{10,... | collective-permute-start | bytes 98312 | tf_op jit(solution)/shard_map/ppermute | solution.py:278
  3.1 3.4 %collective-permute-start.2 = (bf16[8,16,128]{2,1,0:T(8,128)(2,1)S(1)}, bf16[8,16,128]{2,1,0:T(8,128)(2,1)S(1)}, u32[]{:S(2)}, u32[]{:S(2)}) collective-permute-start(bf16[8,16,128]{2,1,0:T(8,128)(2,1)S(1)} %get-tuple-element.20), channel_id=1, source_target_pairs={{0,3},{1,2},{2,1},{3,0},{4,7},{5,6},{6,5},{7,4},{8,11},{9,10},{10,... | collective-permute-start | bytes 98312 | tf_op jit(solution)/shard_map/ppermute | solution.py:278
  29.8 5.7 %collective-permute-start.3 = (bf16[32,16,128]{2,1,0:T(8,128)(2,1)S(1)}, bf16[32,16,128]{2,1,0:T(8,128)(2,1)S(1)}, u32[]{:S(2)}, u32[]{:S(2)}) collective-permute-start(bf16[32,16,128]{2,1,0:T(8,128)(2,1)S(1)} %slice.4), channel_id=1, source_target_pairs={{0,1},{1,0},{2,3},{3,2},{4,5},{5,4},{6,7},{7,6},{8,9},{9,8},{10,11... | collective-permute-start | bytes 393224 | tf_op jit(solution)/shard_map/ppermute | solution.py:307

commit v6 on v5

--- a/solution.py
+++ b/solution.py
@@ -27,11 +27,11 @@
 
 
 def prepare_kernel(
-    all_filters_ref, all_taps_ref, all_skip_ref, all_branches_ref, same_ref, other_ref, taps_ref, skip_ref, branches_ref,
+    all_filters_ref, all_taps_ref, all_skip_ref, all_branches_ref, cast_ref, taps_ref, skip_ref, branches_ref,
     filters_ref, rows_ref, semaphores,
 ):
-    sources = (all_filters_ref, all_taps_ref, all_skip_ref, all_branches_ref)
-    targets = (filters_ref, taps_ref, skip_ref, branches_ref)
+    sources = [all_filters_ref, all_taps_ref, all_skip_ref] + [all_branches_ref.at[branch] for branch in range(3)]
+    targets = [filters_ref, taps_ref, skip_ref] + [branches_ref.at[branch] for branch in range(3)]
     copies = [
         pltpu.make_async_copy(source, target, semaphores.at[at])
         for at, (source, target) in enumerate(zip(sources, targets))
@@ -41,12 +41,20 @@
     copies[0].wait()
     for block in range(BLOCKS):
         rows_ref[pl.ds(block, FILTERS, stride=BLOCKS), :] = filters_ref[:, block * LANES : (block + 1) * LANES]
-    rows = rows_ref[...].reshape(FILTERS // 2, 2, BLOCKS, LANES)
-    second = lax.rem(lax.axis_index("ch"), 2) == 1
-    same_ref[...] = jnp.where(second, rows[:, 1], rows[:, 0]).astype(bf16)
-    other_ref[...] = jnp.where(second, rows[:, 0], rows[:, 1]).astype(bf16)
+    cast_ref[...] = rows_ref[...].reshape(FILTERS, BLOCKS, LANES).astype(bf16)
     for copy in copies[1:]:
         copy.wait()
+
+
+PLACES = [(chip, own) for chip in range(2) for own in range(OWN)]
+
+
+def channel_at(chip, own):
+    return (chip * OWN + own) * FILTERS
+
+
+def part_at(chip):
+    return slice(chip * FILTERS, (chip + 1) * FILTERS)
 
 
 def stand(columns_ref, small_ref, taps_ref, skip_ref):
@@ -102,7 +110,9 @@
         return carry
 
     lax.fori_loop(0, CHANNELS // STEP, body, 0)
-    signal_ref[...] = rows_ref[...].reshape(PARTS, HALF, LANES).astype(bf16)
+    for chip, own in PLACES:
+        rows = rows_ref[channel_at(chip, own) * BLOCKS : (channel_at(chip, own) + FILTERS) * BLOCKS, :]
+        signal_ref[part_at(chip), own * BLOCKS : (own + 1) * BLOCKS, :] = rows.reshape(FILTERS, BLOCKS, LANES).astype(bf16)
     lane = lax.broadcasted_iota(jnp.int32, (CHANNELS, LANES), 1)
     edge = jnp.where(lane < REACH, edges_ref[0], 0.0)
     for branch in range(3):
@@ -120,19 +130,19 @@
     gains = jnp.where(lane < SKIP, 0.0, jnp.where(lane < SKIP + 8, skip_high, skip - skip_high))
     edges_ref[0] = high + pltpu.roll(edge - high, LOW, 1) + gains
     rows_ref[: PARTS * EDGE, :] = jnp.zeros((PARTS * EDGE, LANES), f32)
-    for own in range(OWN):
-        rows_ref[pl.ds(own, PARTS, stride=EDGE), :] = edges_ref[0, pl.ds(own, PARTS, stride=OWN), :]
+    for chip, own in PLACES:
+        begin = channel_at(chip, own)
+        rows_ref[pl.ds(chip * FILTERS * EDGE + own, FILTERS, stride=EDGE), :] = edges_ref[0, begin : begin + FILTERS, :]
     edge_ref[...] = rows_ref[: PARTS * EDGE, :].reshape(PARTS, EDGE, LANES).astype(bf16)
 
 
-def pack_kernel(signal_ref, edge_ref, own_ref, one_ref, two_ref, three_ref, send_ref):
+def pack_kernel(signal_ref, edge_ref, own_ref, other_ref, send_ref):
     send_ref[:, :HALF, :] = signal_ref[...]
     send_ref[:, EDGES_AT:, :] = edge_ref[...]
-    here = lax.axis_index("ch")
-    owned = FILTERS // OWN
-    for apart, taps_from in enumerate((own_ref, one_ref, two_ref, three_ref)):
-        begin = pl.multiple_of((here ^ apart) * owned, owned)
-        send_ref[pl.ds(begin, owned), HALF:EDGES_AT, :] = taps_from[...]
+    chip = lax.div(lax.axis_index("ch"), 2)
+    for at, taps_ref in ((chip, own_ref), (1 - chip, other_ref)):
+        begin = pl.multiple_of(at * FILTERS, FILTERS)
+        send_ref[pl.ds(begin, FILTERS), HALF:EDGES_AT, :] = taps_ref[...]
 
 
 def conv_kernel(data_ref, *rest):
@@ -244,7 +254,9 @@
 
 
 def mix_kernel(conv_ref, query_ref, direct_ref, out_ref, rows_ref):
-    rows_ref[...] = conv_ref[...].reshape(CHANNELS * BLOCKS, LANES).astype(f32)
+    for chip, own in PLACES:
+        rows = conv_ref[part_at(chip), own * BLOCKS : (own + 1) * BLOCKS, :].reshape(FILTERS * BLOCKS, LANES)
+        rows_ref[channel_at(chip, own) * BLOCKS : (channel_at(chip, own) + FILTERS) * BLOCKS, :] = rows.astype(f32)
     for block in range(BLOCKS):
         at = slice(block * LANES, (block + 1) * LANES)
         conv = rows_ref[pl.ds(block, CHANNELS, stride=BLOCKS), :]
@@ -256,27 +268,24 @@
 
 
 def on_device(branches, short_taps, long_filter, skip_gain):
-    same, other, taps, skip, branches = pl.pallas_call(
+    own_filters, taps, skip, branches = pl.pallas_call(
         prepare_kernel,
         out_shape=[
-            jax.ShapeDtypeStruct((FILTERS // 2, BLOCKS, LANES), bf16),
-            jax.ShapeDtypeStruct((FILTERS // 2, BLOCKS, LANES), bf16),
+            jax.ShapeDtypeStruct((FILTERS, BLOCKS, LANES), bf16),
             jax.ShapeDtypeStruct((3, TAPS, CHANNELS), f32),
             jax.ShapeDtypeStruct((1, CHANNELS), f32),
             jax.ShapeDtypeStruct((3, CHANNELS, TOKENS), bf16),
         ],
         in_specs=[pl.BlockSpec(memory_space=pltpu.HBM)] * 4,
-        out_specs=[VMEM] * 5,
+        out_specs=[VMEM] * 4,
         scratch_shapes=[
             pltpu.VMEM((FILTERS, TOKENS), f32),
             pltpu.VMEM((FILTERS * BLOCKS, LANES), f32),
-            pltpu.SemaphoreType.DMA((4,)),
+            pltpu.SemaphoreType.DMA((6,)),
         ],
         compiler_params=pltpu.CompilerParams(vmem_limit_bytes=8 * 2**20),
     )(in_hbm(long_filter), in_hbm(short_taps.transpose(0, 2, 1)), in_hbm(skip_gain[None, :]), in_hbm(branches))
-    filters = [same] + [
-        lax.ppermute(sent, "ch", [(i, i ^ apart) for i in range(4)]) for apart, sent in ((1, other), (2, same), (3, other))
-    ]
+    other_filters = lax.ppermute(own_filters, "ch", [(i, i ^ 2) for i in range(4)])
     signal, edge, query, direct = pl.pallas_call(
         short_kernel,
         out_shape=[
@@ -299,10 +308,10 @@
     send = pl.pallas_call(
         pack_kernel,
         out_shape=jax.ShapeDtypeStruct((PARTS, EDGES_AT + EDGE, LANES), bf16),
-        in_specs=[VMEM] * 6,
+        in_specs=[VMEM] * 4,
         out_specs=VMEM,
         compiler_params=pltpu.CompilerParams(vmem_limit_bytes=16 * 2**20),
-    )(signal, edge, *filters)
+    )(signal, edge, own_filters, other_filters)
     data = lax.all_to_all(send, "ctx", 0, 0, tiled=True)
     swapped = lax.ppermute(data[:, HALF:EDGES_AT, :], "ch", [(i, i ^ 1) for i in range(4)])
     conv = convolve(data, swapped, convolve(data))

time: 57.2 us -> 55.6 us (0.972)
  blocking collectives: 38.3 us -> 37.7 us
    all_to_all x1, blocking collectives: 23.2 us -> 22.6 us  [on_device(): data = lax.all_to_all(send, 'ctx', 0, 0, tiled=True)]
    ppermute x3 -> x1, starting transfers between devices: 1.95 us -> 1.74 us  [on_device(): lax.ppermute(own_filters, 'ch', [(i, i ^ 2) for i in range(4)])]
  transfers between devices with their start and end apart: 4 -> 2, of which waited for: 1 -> 0; matrix products, arithmetic and copies ran while one was open for 0% -> 0% of each run, Pallas kernels for 14% -> 15%
where the time goes in v6:
time: 55.6 us; the launch traced here: 55.4 us
  blocking collectives  37.7 us (68%)
  Pallas kernels  15.9 us (29%)
  starting transfers between devices  1.82 us (3%)
    all_to_all x1, blocking collectives, on_device(): data = lax.all_to_all(send, 'ctx', 0, 0, tiled=True)  22.6 us
    all_to_all x1, blocking collectives, on_device(): conv = lax.all_to_all(conv, 'ctx', 0, 0, tiled=True)  15.1 us
    pallas_call x2, Pallas kernels, convolve(): pl.pallas_call(conv_kernel, out_shape=jax.ShapeDtypeStruct((PARTS, HALF i...  10.9 us
    pallas_call x1, Pallas kernels, on_device(): pl.pallas_call(short_kernel, out_shape=[jax.ShapeDtypeStruct((PARTS, HALF...  2.67 us
    ppermute x1, starting transfers between devices, on_device(): lax.ppermute(own_filters, 'ch', [(i, i ^ 2) for i in range(4)])  1.74 us
    pallas_call x1, Pallas kernels, on_device(): pl.pallas_call(prepare_kernel, out_shape=[jax.ShapeDtypeStruct((FILTERS,...  1.26 us
  transfers between devices with their start and end apart: 2, of which 0 were waited for; matrix products, arithmetic and copies ran while one was open for 0% of the time, Pallas kernels for 15%

profile of v6, /device:TPU:0, one launch (start us, length us, event | category | flops | bytes accessed | tf_op | source)
XLA Modules:
  0.0 55.4 jit_solution(6865755286560529134)
XLA Ops:
  0.0 1.3 %shard_map.46 = (bf16[16,16,128]{2,1,0:T(8,128)(2,1)S(1)}, f32[3,7,64]{2,1,0:T(8,128)S(1)}, f32[1,64]{1,0:T(1,128)S(1)}, bf16[3,64,2048]{2,1,0:T(8,128)(2,1)S(1)}) custom-call(f32[16,2048]{1,0:T(8,128)} %all_filters_ref.1, f32[3,7,64]{2,1,0:T(8,128)} %bitcast.2, f32[1,64]{1,0:T(1,128)} %bitcast.3, bf16[3,64,2048]{2,1,0:T(8,128)(2,1)} %all_branches_ref.1), custom_call_target="tpu_custom_call" | custom-call | tf_op jit(solution)/shard_map/pallas_call | solution.py:271
  1.3 1.7 %collective-permute-start = (bf16[16,16,128]{2,1,0:T(8,128)(2,1)S(1)}, bf16[16,16,128]{2,1,0:T(8,128)(2,1)S(1)}, u32[]{:S(2)}, u32[]{:S(2)}) collective-permute-start(bf16[16,16,128]{2,1,0:T(8,128)(2,1)S(1)} %get-tuple-element.18.own_ref), channel_id=1, source_target_pairs={{0,2},{1,3},{2,0},{3,1},{4,6},{5,7},{6,4},{7,5},{8,10},{9,11},{10,... | collective-permute-start | bytes 196616 | tf_op jit(solution)/shard_map/ppermute | solution.py:288
  3.0 2.7 %shard_map.47 = (bf16[32,32,128]{2,1,0:T(8,128)(2,1)S(1)}, bf16[32,8,128]{2,1,0:T(8,128)(2,1)S(1)}, f32[64,2048]{1,0:T(8,128)S(1)}, f32[64,2048]{1,0:T(8,128)S(1)}) custom-call(bf16[3,64,2048]{2,1,0:T(8,128)(2,1)S(1)} %get-tuple-element.13.branch_ref, f32[3,7,64]{2,1,0:T(8,128)S(1)} %get-tuple-element.14.taps_ref, f32[1,64]{1,0:T(1,128)S(1)} %get-tuple-element.15.skip_ref), custom_call_target="tpu_custom_call" | custom-call | flops 10000000 | bytes 8388608 | tf_op jit(solution)/shard_map/pallas_call | solution.py:289
  5.7 0.0 collective-permute-done.other_ref
  5.7 22.6 %all_to_all.10.data_ref = bf16[32,56,128]{2,1,0:T(8,128)(2,1)S(1)} all-to-all(bf16[32,56,128]{2,1,0:T(8,128)(2,1)S(1)} %shard_map.48), channel_id=1, replica_groups=mesh['ctx'=32,'ch'=4] {'ctx'}, dimensions={0} | all-to-all | bytes 917504 | tf_op jit(solution)/shard_map/all_to_all | solution.py:315
  28.3 0.1 collective-permute-start.1
  28.4 5.4 %shard_map.49.rest_1_ = bf16[32,16,128]{2,1,0:T(8,128)(2,1)S(1)} custom-call(bf16[32,56,128]{2,1,0:T(8,128)(2,1)S(1)} %all_to_all.10.data_ref), custom_call_target="tpu_custom_call" | custom-call | flops 4000000000 | bytes 1048576 | tf_op jit(solution)/shard_map/pallas_call | solution.py:237
  33.9 0.0 collective-permute-done.1.rest_0_
  33.9 5.4 %shard_map.50 = bf16[32,32,128]{2,1,0:T(8,128)(2,1)S(1)} custom-call(bf16[32,56,128]{2,1,0:T(8,128)(2,1)S(1)} %all_to_all.10.data_ref, bf16[32,16,128]{2,1,0:T(8,128)(2,1)S(1)} %collective-permute-done.1.rest_0_, bf16[32,16,128]{2,1,0:T(8,128)(2,1)S(1)} %shard_map.49.rest_1_), custom_call_target="tpu_custom_call" | custom-call | flops 4000000000 | bytes 1048576 | tf_op jit(solution)/shard_map/pallas_call | solution.py:237
  39.3 15.1 %all_to_all.11.conv_ref = bf16[32,32,128]{2,1,0:T(8,128)(2,1)S(1)} all-to-all(bf16[32,32,128]{2,1,0:T(8,128)(2,1)S(1)} %shard_map.50), channel_id=1, replica_groups=mesh['ctx'=32,'ch'=4] {'ctx'}, dimensions={0} | all-to-all | bytes 524288 | tf_op jit(solution)/shard_map/all_to_all | solution.py:318
  54.4 1.0 %shard_map.51 = bf16[64,2048]{1,0:T(8,128)(2,1)} custom-call(bf16[32,32,128]{2,1,0:T(8,128)(2,1)S(1)} %all_to_all.11.conv_ref, f32[64,2048]{1,0:T(8,128)S(1)} %get-tuple-element.19.query_ref, f32[64,2048]{1,0:T(8,128)S(1)} %get-tuple-element.20.direct_ref), custom_call_target="tpu_custom_call" | custom-call | tf_op jit(solution)/shard_map/pallas_call | solution.py:319
  (2 shorter events, 0.0 us)
Async XLA Ops:
  1.3 4.4 %collective-permute-start = (bf16[16,16,128]{2,1,0:T(8,128)(2,1)S(1)}, bf16[16,16,128]{2,1,0:T(8,128)(2,1)S(1)}, u32[]{:S(2)}, u32[]{:S(2)}) collective-permute-start(bf16[16,16,128]{2,1,0:T(8,128)(2,1)S(1)} %get-tuple-element.18.own_ref), channel_id=1, source_target_pairs={{0,2},{1,3},{2,0},{3,1},{4,6},{5,7},{6,4},{7,5},{8,10},{9,11},{10,... | collective-permute-start | bytes 196616 | tf_op jit(solution)/shard_map/ppermute | solution.py:288
  28.3 5.5 %collective-permute-start.1 = (bf16[32,16,128]{2,1,0:T(8,128)(2,1)S(1)}, bf16[32,16,128]{2,1,0:T(8,128)(2,1)S(1)}, u32[]{:S(2)}, u32[]{:S(2)}) collective-permute-start(bf16[32,16,128]{2,1,0:T(8,128)(2,1)S(1)} %slice.4), channel_id=1, source_target_pairs={{0,1},{1,0},{2,3},{3,2},{4,5},{5,4},{6,7},{7,6},{8,9},{9,8},{10,11... | collective-permute-start | bytes 393224 | tf_op jit(solution)/shard_map/ppermute | solution.py:316

commit v7 on v6

--- a/solution.py
+++ b/solution.py
@@ -41,7 +41,7 @@
     copies[0].wait()
     for block in range(BLOCKS):
         rows_ref[pl.ds(block, FILTERS, stride=BLOCKS), :] = filters_ref[:, block * LANES : (block + 1) * LANES]
-    cast_ref[...] = rows_ref[...].reshape(FILTERS, BLOCKS, LANES).astype(bf16)
+    cast_ref[...] = rows_ref[: FILTERS * BLOCKS, :].reshape(FILTERS, BLOCKS, LANES).astype(bf16)
     for copy in copies[1:]:
         copy.wait()
 
@@ -159,7 +159,7 @@
     previous = jnp.zeros((WIDTH, LANES), bf16)
     first = lax.broadcasted_iota(jnp.int32, (PARTS, LANES), 1) < REACH
     start = lax.broadcasted_iota(jnp.int32, (PARTS, LANES), 0) == 0
-    edge_ref[...] = data_ref[:, EDGES_AT:, :].reshape(PARTS * EDGE, LANES).astype(f32)
+    edge_ref[: PARTS * EDGE, :] = data_ref[:, EDGES_AT:, :].reshape(PARTS * EDGE, LANES).astype(f32)
     opening = pl.ds(shift, PARTS, stride=BLOCKS)
 
     def turn_back(value, by):
@@ -242,7 +242,7 @@
         scratch_shapes=[
             pltpu.VMEM((2 * GROUP + ROWS, LANES), f32),
             pltpu.VMEM((ROWS, LANES), f32),
-            pltpu.VMEM((PARTS * EDGE, LANES), f32),
+            pltpu.VMEM((PARTS * EDGE + EDGE, LANES), f32),
             pltpu.VMEM((2, ROWS, GROUP * WIDTH), bf16),
             pltpu.VMEM((GROUP * WIDTH, 2 * LANES), bf16),
             pltpu.VMEM((GROUP * WIDTH, 2 * LANES), bf16),
@@ -253,14 +253,22 @@
     )(data, *inputs)
 
 
-def mix_kernel(conv_ref, query_ref, direct_ref, out_ref, rows_ref):
+def mix_kernel(conv_ref, query_ref, direct_ref, out_ref, rows_ref, mixed_ref, semaphores):
+    copies = []
     for chip, own in PLACES:
+        begin = channel_at(chip, own)
+        channels = slice(begin, begin + FILTERS)
         rows = conv_ref[part_at(chip), own * BLOCKS : (own + 1) * BLOCKS, :].reshape(FILTERS * BLOCKS, LANES)
-        rows_ref[channel_at(chip, own) * BLOCKS : (channel_at(chip, own) + FILTERS) * BLOCKS, :] = rows.astype(f32)
-    for block in range(BLOCKS):
-        at = slice(block * LANES, (block + 1) * LANES)
-        conv = rows_ref[pl.ds(block, CHANNELS, stride=BLOCKS), :]
-        out_ref[:, at] = (query_ref[:, at] * conv + direct_ref[:, at]).astype(bf16)
+        rows_ref[begin * BLOCKS : (begin + FILTERS) * BLOCKS, :] = rows.astype(f32)
+        for block in range(BLOCKS):
+            at = slice(block * LANES, (block + 1) * LANES)
+            conv = rows_ref[pl.ds(begin * BLOCKS + block, FILTERS, stride=BLOCKS), :]
+            mixed_ref[channels, at] = (query_ref[channels, at] * conv + direct_ref[channels, at]).astype(bf16)
+        slot = len(copies)
+        copies.append(pltpu.make_async_copy(mixed_ref.at[channels, :], out_ref.at[channels, :], semaphores.at[slot]))
+        copies[-1].start()
+    for copy in copies:
+        copy.wait()
 
 
 def in_hbm(array):
@@ -280,7 +288,7 @@
         out_specs=[VMEM] * 4,
         scratch_shapes=[
             pltpu.VMEM((FILTERS, TOKENS), f32),
-            pltpu.VMEM((FILTERS * BLOCKS, LANES), f32),
+            pltpu.VMEM((FILTERS * BLOCKS + BLOCKS, LANES), f32),
             pltpu.SemaphoreType.DMA((6,)),
         ],
         compiler_params=pltpu.CompilerParams(vmem_limit_bytes=8 * 2**20),
@@ -297,7 +305,7 @@
         in_specs=[VMEM] * 3,
         out_specs=[VMEM] * 4,
         scratch_shapes=[
-            pltpu.VMEM((CHANNELS * BLOCKS, LANES), f32),
+            pltpu.VMEM((CHANNELS * BLOCKS + BLOCKS, LANES), f32),
             pltpu.VMEM((3, CHANNELS, LANES), f32),
             pltpu.VMEM((LANES, LANES), f32),
             pltpu.VMEM((LANES, LANES), f32),
@@ -320,8 +328,12 @@
         mix_kernel,
         out_shape=jax.ShapeDtypeStruct((CHANNELS, TOKENS), bf16),
         in_specs=[VMEM] * 3,
-        out_specs=VMEM,
-        scratch_shapes=[pltpu.VMEM((CHANNELS * BLOCKS, LANES), f32)],
+        out_specs=pl.BlockSpec(memory_space=pltpu.HBM),
+        scratch_shapes=[
+            pltpu.VMEM((CHANNELS * BLOCKS + BLOCKS, LANES), f32),
+            pltpu.VMEM((CHANNELS, TOKENS), bf16),
+            pltpu.SemaphoreType.DMA((len(PLACES),)),
+        ],
         compiler_params=pltpu.CompilerParams(vmem_limit_bytes=32 * 2**20),
     )(conv, query, direct)
 

time: 55.6 us -> 55.5 us (level)
  no operation moved by 1% of the time
where the time goes in v7:
time: 55.5 us; the launch traced here: 55.3 us
  blocking collectives  37.7 us (68%)
  Pallas kernels  15.8 us (28%)
  starting transfers between devices  1.82 us (3%)
    all_to_all x1, blocking collectives, on_device(): data = lax.all_to_all(send, 'ctx', 0, 0, tiled=True)  22.6 us
    all_to_all x1, blocking collectives, on_device(): conv = lax.all_to_all(conv, 'ctx', 0, 0, tiled=True)  15.1 us
    pallas_call x2, Pallas kernels, convolve(): pl.pallas_call(conv_kernel, out_shape=jax.ShapeDtypeStruct((PARTS, HALF i...  10.9 us
    pallas_call x1, Pallas kernels, on_device(): pl.pallas_call(short_kernel, out_shape=[jax.ShapeDtypeStruct((PARTS, HALF...  2.67 us
    ppermute x1, starting transfers between devices, on_device(): lax.ppermute(own_filters, 'ch', [(i, i ^ 2) for i in range(4)])  1.74 us
    pallas_call x1, Pallas kernels, on_device(): pl.pallas_call(prepare_kernel, out_shape=[jax.ShapeDtypeStruct((FILTERS,...  1.26 us
  transfers between devices with their start and end apart: 2, of which 0 were waited for; matrix products, arithmetic and copies ran while one was open for 0% of the time, Pallas kernels for 15%

profile of v7, /device:TPU:0, one launch (start us, length us, event | category | flops | bytes accessed | tf_op | source)
XLA Modules:
  0.0 55.3 jit_solution(3860395739432332736)
XLA Ops:
  0.0 1.3 %shard_map.46 = (bf16[16,16,128]{2,1,0:T(8,128)(2,1)S(1)}, f32[3,7,64]{2,1,0:T(8,128)S(1)}, f32[1,64]{1,0:T(1,128)S(1)}, bf16[3,64,2048]{2,1,0:T(8,128)(2,1)S(1)}) custom-call(f32[16,2048]{1,0:T(8,128)} %all_filters_ref.1, f32[3,7,64]{2,1,0:T(8,128)} %bitcast.2, f32[1,64]{1,0:T(1,128)} %bitcast.3, bf16[3,64,2048]{2,1,0:T(8,128)(2,1)} %all_branches_ref.1), custom_call_target="tpu_custom_call" | custom-call | tf_op jit(solution)/shard_map/pallas_call | solution.py:279
  1.3 1.7 %collective-permute-start = (bf16[16,16,128]{2,1,0:T(8,128)(2,1)S(1)}, bf16[16,16,128]{2,1,0:T(8,128)(2,1)S(1)}, u32[]{:S(2)}, u32[]{:S(2)}) collective-permute-start(bf16[16,16,128]{2,1,0:T(8,128)(2,1)S(1)} %get-tuple-element.18.own_ref), channel_id=1, source_target_pairs={{0,2},{1,3},{2,0},{3,1},{4,6},{5,7},{6,4},{7,5},{8,10},{9,11},{10,... | collective-permute-start | bytes 196616 | tf_op jit(solution)/shard_map/ppermute | solution.py:296
  3.0 2.7 %shard_map.47 = (bf16[32,32,128]{2,1,0:T(8,128)(2,1)S(1)}, bf16[32,8,128]{2,1,0:T(8,128)(2,1)S(1)}, f32[64,2048]{1,0:T(8,128)S(1)}, f32[64,2048]{1,0:T(8,128)S(1)}) custom-call(bf16[3,64,2048]{2,1,0:T(8,128)(2,1)S(1)} %get-tuple-element.13.branch_ref, f32[3,7,64]{2,1,0:T(8,128)S(1)} %get-tuple-element.14.taps_ref, f32[1,64]{1,0:T(1,128)S(1)} %get-tuple-element.15.skip_ref), custom_call_target="tpu_custom_call" | custom-call | flops 10000000 | bytes 8388608 | tf_op jit(solution)/shard_map/pallas_call | solution.py:297
  5.7 0.0 collective-permute-done.other_ref
  5.7 22.6 %all_to_all.10.data_ref = bf16[32,56,128]{2,1,0:T(8,128)(2,1)S(1)} all-to-all(bf16[32,56,128]{2,1,0:T(8,128)(2,1)S(1)} %shard_map.48), channel_id=1, replica_groups=mesh['ctx'=32,'ch'=4] {'ctx'}, dimensions={0} | all-to-all | bytes 917504 | tf_op jit(solution)/shard_map/all_to_all | solution.py:323
  28.3 0.1 collective-permute-start.1
  28.4 5.4 %shard_map.49.rest_1_ = bf16[32,16,128]{2,1,0:T(8,128)(2,1)S(1)} custom-call(bf16[32,56,128]{2,1,0:T(8,128)(2,1)S(1)} %all_to_all.10.data_ref), custom_call_target="tpu_custom_call" | custom-call | flops 4000000000 | bytes 1048576 | tf_op jit(solution)/shard_map/pallas_call | solution.py:237
  33.8 0.0 collective-permute-done.1.rest_0_
  33.9 5.4 %shard_map.50 = bf16[32,32,128]{2,1,0:T(8,128)(2,1)S(1)} custom-call(bf16[32,56,128]{2,1,0:T(8,128)(2,1)S(1)} %all_to_all.10.data_ref, bf16[32,16,128]{2,1,0:T(8,128)(2,1)S(1)} %collective-permute-done.1.rest_0_, bf16[32,16,128]{2,1,0:T(8,128)(2,1)S(1)} %shard_map.49.rest_1_), custom_call_target="tpu_custom_call" | custom-call | flops 4000000000 | bytes 1048576 | tf_op jit(solution)/shard_map/pallas_call | solution.py:237
  39.3 15.1 %all_to_all.11.conv_ref = bf16[32,32,128]{2,1,0:T(8,128)(2,1)S(1)} all-to-all(bf16[32,32,128]{2,1,0:T(8,128)(2,1)S(1)} %shard_map.50), channel_id=1, replica_groups=mesh['ctx'=32,'ch'=4] {'ctx'}, dimensions={0} | all-to-all | bytes 524288 | tf_op jit(solution)/shard_map/all_to_all | solution.py:326
  54.4 0.9 %shard_map.51 = bf16[64,2048]{1,0:T(8,128)(2,1)} custom-call(bf16[32,32,128]{2,1,0:T(8,128)(2,1)S(1)} %all_to_all.11.conv_ref, f32[64,2048]{1,0:T(8,128)S(1)} %get-tuple-element.19.query_ref, f32[64,2048]{1,0:T(8,128)S(1)} %get-tuple-element.20.direct_ref), custom_call_target="tpu_custom_call" | custom-call | tf_op jit(solution)/shard_map/pallas_call | solution.py:327
  (2 shorter events, 0.0 us)
Async XLA Ops:
  1.3 4.4 %collective-permute-start = (bf16[16,16,128]{2,1,0:T(8,128)(2,1)S(1)}, bf16[16,16,128]{2,1,0:T(8,128)(2,1)S(1)}, u32[]{:S(2)}, u32[]{:S(2)}) collective-permute-start(bf16[16,16,128]{2,1,0:T(8,128)(2,1)S(1)} %get-tuple-element.18.own_ref), channel_id=1, source_target_pairs={{0,2},{1,3},{2,0},{3,1},{4,6},{5,7},{6,4},{7,5},{8,10},{9,11},{10,... | collective-permute-start | bytes 196616 | tf_op jit(solution)/shard_map/ppermute | solution.py:296
  28.3 5.5 %collective-permute-start.1 = (bf16[32,16,128]{2,1,0:T(8,128)(2,1)S(1)}, bf16[32,16,128]{2,1,0:T(8,128)(2,1)S(1)}, u32[]{:S(2)}, u32[]{:S(2)}) collective-permute-start(bf16[32,16,128]{2,1,0:T(8,128)(2,1)S(1)} %slice.4), channel_id=1, source_target_pairs={{0,1},{1,0},{2,3},{3,2},{4,5},{5,4},{6,7},{7,6},{8,9},{9,8},{10,11... | collective-permute-start | bytes 393224 | tf_op jit(solution)/shard_map/ppermute | solution.py:324

commit v8 on v7

--- a/solution.py
+++ b/solution.py
@@ -27,8 +27,8 @@
 
 
 def prepare_kernel(
-    all_filters_ref, all_taps_ref, all_skip_ref, all_branches_ref, cast_ref, taps_ref, skip_ref, branches_ref,
-    filters_ref, rows_ref, semaphores,
+    all_filters_ref, all_taps_ref, all_skip_ref, all_branches_ref, cast_ref, columns_ref, branches_ref,
+    filters_ref, taps_ref, skip_ref, small_ref, rows_ref, semaphores,
 ):
     sources = [all_filters_ref, all_taps_ref, all_skip_ref] + [all_branches_ref.at[branch] for branch in range(3)]
     targets = [filters_ref, taps_ref, skip_ref] + [branches_ref.at[branch] for branch in range(3)]
@@ -42,7 +42,10 @@
     for block in range(BLOCKS):
         rows_ref[pl.ds(block, FILTERS, stride=BLOCKS), :] = filters_ref[:, block * LANES : (block + 1) * LANES]
     cast_ref[...] = rows_ref[: FILTERS * BLOCKS, :].reshape(FILTERS, BLOCKS, LANES).astype(bf16)
-    for copy in copies[1:]:
+    for copy in copies[1:3]:
+        copy.wait()
+    stand(columns_ref, small_ref, taps_ref, skip_ref)
+    for copy in copies[3:]:
         copy.wait()
 
 
@@ -80,9 +83,8 @@
 
 
 def short_kernel(
-    branch_ref, taps_ref, skip_ref, signal_ref, edge_ref, query_ref, direct_ref, rows_ref, edges_ref, small_ref, columns_ref
+    branch_ref, columns_ref, signal_ref, edge_ref, query_ref, direct_ref, rows_ref, edges_ref
 ):
-    stand(columns_ref, small_ref, taps_ref, skip_ref)
     first = lax.broadcasted_iota(jnp.int32, (STEP, LANES), 1) < REACH
 
     def body(index, carry):
@@ -276,18 +278,20 @@
 
 
 def on_device(branches, short_taps, long_filter, skip_gain):
-    own_filters, taps, skip, branches = pl.pallas_call(
+    own_filters, columns, branches = pl.pallas_call(
         prepare_kernel,
         out_shape=[
             jax.ShapeDtypeStruct((FILTERS, BLOCKS, LANES), bf16),
-            jax.ShapeDtypeStruct((3, TAPS, CHANNELS), f32),
-            jax.ShapeDtypeStruct((1, CHANNELS), f32),
+            jax.ShapeDtypeStruct((LANES, LANES), f32),
             jax.ShapeDtypeStruct((3, CHANNELS, TOKENS), bf16),
         ],
         in_specs=[pl.BlockSpec(memory_space=pltpu.HBM)] * 4,
-        out_specs=[VMEM] * 4,
+        out_specs=[VMEM] * 3,
         scratch_shapes=[
             pltpu.VMEM((FILTERS, TOKENS), f32),
+            pltpu.VMEM((3, TAPS, CHANNELS), f32),
+            pltpu.VMEM((1, CHANNELS), f32),
+            pltpu.VMEM((LANES, LANES), f32),
             pltpu.VMEM((FILTERS * BLOCKS + BLOCKS, LANES), f32),
             pltpu.SemaphoreType.DMA((6,)),
         ],
@@ -302,17 +306,15 @@
             jax.ShapeDtypeStruct((CHANNELS, TOKENS), f32),
             jax.ShapeDtypeStruct((CHANNELS, TOKENS), f32),
         ],
-        in_specs=[VMEM] * 3,
+        in_specs=[VMEM] * 2,
         out_specs=[VMEM] * 4,
         scratch_shapes=[
             pltpu.VMEM((CHANNELS * BLOCKS + BLOCKS, LANES), f32),
             pltpu.VMEM((3, CHANNELS, LANES), f32),
-            pltpu.VMEM((LANES, LANES), f32),
-            pltpu.VMEM((LANES, LANES), f32),
         ],
         compiler_params=pltpu.CompilerParams(vmem_limit_bytes=16 * 2**20),
         cost_estimate=pl.CostEstimate(flops=10**7, bytes_accessed=8 * 2**20, transcendentals=0),
-    )(branches, taps, skip)
+    )(branches, columns)
     send = pl.pallas_call(
         pack_kernel,
         out_shape=jax.ShapeDtypeStruct((PARTS, EDGES_AT + EDGE, LANES), bf16),

time: 55.5 us -> 55.4 us (level)
  transfers between devices with their start and end apart: 2 -> 2, of which waited for: 0 -> 0; matrix products, arithmetic and copies ran while one was open for 0% -> 0% of each run, Pallas kernels for 15% -> 14%
where the time goes in v8:
time: 55.4 us; the launch traced here: 55.2 us
  blocking collectives  37.6 us (68%)
  Pallas kernels  15.6 us (28%)
  starting transfers between devices  1.82 us (3%)
    all_to_all x1, blocking collectives, on_device(): data = lax.all_to_all(send, 'ctx', 0, 0, tiled=True)  22.5 us
    all_to_all x1, blocking collectives, on_device(): conv = lax.all_to_all(conv, 'ctx', 0, 0, tiled=True)  15.1 us
    pallas_call x2, Pallas kernels, convolve(): pl.pallas_call(conv_kernel, out_shape=jax.ShapeDtypeStruct((PARTS, HALF i...  10.9 us
    pallas_call x1, Pallas kernels, on_device(): pl.pallas_call(short_kernel, out_shape=[jax.ShapeDtypeStruct((PARTS, HALF...  2.55 us
    ppermute x1, starting transfers between devices, on_device(): lax.ppermute(own_filters, 'ch', [(i, i ^ 2) for i in range(4)])  1.74 us
    pallas_call x1, Pallas kernels, on_device(): pl.pallas_call(prepare_kernel, out_shape=[jax.ShapeDtypeStruct((FILTERS,...  1.26 us
  transfers between devices with their start and end apart: 2, of which 0 were waited for; matrix products, arithmetic and copies ran while one was open for 0% of the time, Pallas kernels for 14%

profile of v8, /device:TPU:0, one launch (start us, length us, event | category | flops | bytes accessed | tf_op | source)
XLA Modules:
  0.0 55.2 jit_solution(17858142461101986697)
XLA Ops:
  0.0 1.3 %shard_map.46 = (bf16[16,16,128]{2,1,0:T(8,128)(2,1)S(1)}, f32[128,128]{1,0:T(8,128)S(1)}, bf16[3,64,2048]{2,1,0:T(8,128)(2,1)S(1)}) custom-call(f32[16,2048]{1,0:T(8,128)} %all_filters_ref.1, f32[3,7,64]{2,1,0:T(8,128)} %bitcast.2, f32[1,64]{1,0:T(1,128)} %bitcast.3, bf16[3,64,2048]{2,1,0:T(8,128)(2,1)} %all_branches_ref.1), custom_call_target="tpu_custom_call" | custom-call | tf_op jit(solution)/shard_map/pallas_call | solution.py:281
  1.3 1.7 %collective-permute-start = (bf16[16,16,128]{2,1,0:T(8,128)(2,1)S(1)}, bf16[16,16,128]{2,1,0:T(8,128)(2,1)S(1)}, u32[]{:S(2)}, u32[]{:S(2)}) collective-permute-start(bf16[16,16,128]{2,1,0:T(8,128)(2,1)S(1)} %get-tuple-element.16.own_ref), channel_id=1, source_target_pairs={{0,2},{1,3},{2,0},{3,1},{4,6},{5,7},{6,4},{7,5},{8,10},{9,11},{10,... | collective-permute-start | bytes 196616 | tf_op jit(solution)/shard_map/ppermute | solution.py:300
  3.0 2.6 %shard_map.47 = (bf16[32,32,128]{2,1,0:T(8,128)(2,1)S(1)}, bf16[32,8,128]{2,1,0:T(8,128)(2,1)S(1)}, f32[64,2048]{1,0:T(8,128)S(1)}, f32[64,2048]{1,0:T(8,128)S(1)}) custom-call(bf16[3,64,2048]{2,1,0:T(8,128)(2,1)S(1)} %get-tuple-element.12.branch_ref, f32[128,128]{1,0:T(8,128)S(1)} %get-tuple-element.13.columns_ref), custom_call_target="tpu_custom_call" | custom-call | flops 10000000 | bytes 8388608 | tf_op jit(solution)/shard_map/pallas_call | solution.py:301
  5.6 0.0 collective-permute-done.other_ref
  5.7 22.5 %all_to_all.10.data_ref = bf16[32,56,128]{2,1,0:T(8,128)(2,1)S(1)} all-to-all(bf16[32,56,128]{2,1,0:T(8,128)(2,1)S(1)} %shard_map.48), channel_id=1, replica_groups=mesh['ctx'=32,'ch'=4] {'ctx'}, dimensions={0} | all-to-all | bytes 917504 | tf_op jit(solution)/shard_map/all_to_all | solution.py:325
  28.2 0.1 collective-permute-start.1
  28.3 5.4 %shard_map.49.rest_1_ = bf16[32,16,128]{2,1,0:T(8,128)(2,1)S(1)} custom-call(bf16[32,56,128]{2,1,0:T(8,128)(2,1)S(1)} %all_to_all.10.data_ref), custom_call_target="tpu_custom_call" | custom-call | flops 4000000000 | bytes 1048576 | tf_op jit(solution)/shard_map/pallas_call | solution.py:239
  33.7 0.0 collective-permute-done.1.rest_0_
  33.7 5.4 %shard_map.50 = bf16[32,32,128]{2,1,0:T(8,128)(2,1)S(1)} custom-call(bf16[32,56,128]{2,1,0:T(8,128)(2,1)S(1)} %all_to_all.10.data_ref, bf16[32,16,128]{2,1,0:T(8,128)(2,1)S(1)} %collective-permute-done.1.rest_0_, bf16[32,16,128]{2,1,0:T(8,128)(2,1)S(1)} %shard_map.49.rest_1_), custom_call_target="tpu_custom_call" | custom-call | flops 4000000000 | bytes 1048576 | tf_op jit(solution)/shard_map/pallas_call | solution.py:239
  39.2 15.1 %all_to_all.11.conv_ref = bf16[32,32,128]{2,1,0:T(8,128)(2,1)S(1)} all-to-all(bf16[32,32,128]{2,1,0:T(8,128)(2,1)S(1)} %shard_map.50), channel_id=1, replica_groups=mesh['ctx'=32,'ch'=4] {'ctx'}, dimensions={0} | all-to-all | bytes 524288 | tf_op jit(solution)/shard_map/all_to_all | solution.py:328
  54.3 0.9 %shard_map.51 = bf16[64,2048]{1,0:T(8,128)(2,1)} custom-call(bf16[32,32,128]{2,1,0:T(8,128)(2,1)S(1)} %all_to_all.11.conv_ref, f32[64,2048]{1,0:T(8,128)S(1)} %get-tuple-element.17.query_ref, f32[64,2048]{1,0:T(8,128)S(1)} %get-tuple-element.18.direct_ref), custom_call_target="tpu_custom_call" | custom-call | tf_op jit(solution)/shard_map/pallas_call | solution.py:329
  (2 shorter events, 0.0 us)
Async XLA Ops:
  1.3 4.3 %collective-permute-start = (bf16[16,16,128]{2,1,0:T(8,128)(2,1)S(1)}, bf16[16,16,128]{2,1,0:T(8,128)(2,1)S(1)}, u32[]{:S(2)}, u32[]{:S(2)}) collective-permute-start(bf16[16,16,128]{2,1,0:T(8,128)(2,1)S(1)} %get-tuple-element.16.own_ref), channel_id=1, source_target_pairs={{0,2},{1,3},{2,0},{3,1},{4,6},{5,7},{6,4},{7,5},{8,10},{9,11},{10,... | collective-permute-start | bytes 196616 | tf_op jit(solution)/shard_map/ppermute | solution.py:300
  28.2 5.5 %collective-permute-start.1 = (bf16[32,16,128]{2,1,0:T(8,128)(2,1)S(1)}, bf16[32,16,128]{2,1,0:T(8,128)(2,1)S(1)}, u32[]{:S(2)}, u32[]{:S(2)}) collective-permute-start(bf16[32,16,128]{2,1,0:T(8,128)(2,1)S(1)} %slice.4), channel_id=1, source_target_pairs={{0,1},{1,0},{2,3},{3,2},{4,5},{5,4},{6,7},{7,6},{8,9},{9,8},{10,11... | collective-permute-start | bytes 393224 | tf_op jit(solution)/shard_map/ppermute | solution.py:326
